TPU v7x, 32 devices: a whole 2x2x4 slice. The times are simulated.
32 devices in a mesh: zg: 4 (over z), zl: 8 (over y, x, core).
Axes of the slice: x: 2, y: 2, z: 4, core: 2. Of those that a mesh axis runs over, the one named last changes fastest.
Arguments:
- brick_data: float32 [512, 16, 256], P(('zg', 'zl')), may hold values from -6 to 6
- brick_xy: int32 [2, 512], P(None, ('zg', 'zl')), may hold values from 0 to 31, as said below
- brick_live: int32 [1, 32], P(None, ('zg', 'zl')), may hold values from 1 to 16, as said below
Outputs:
- pressure_real: float32 [64, 257, 512], P(('zg', 'zl'))
- pressure_imag: float32 [64, 257, 512], P(('zg', 'zl'))
Inputs may be any that keep to these rules, and one draw needn't show every extreme that they name: brick_live[q, d] counts the live slots of owner d in layer q; the live ones are the first; in every layer some owner has all 16 slots live. `brick_xy`: all slots of one brick layer of one z group (live or not) sit at distinct brick positions.
All inputs are finite; a program needn't handle non-finite values.
Results may differ from a plain program's by a relative error of at most 0.00011.
Values sent between devices are 32-bit elements; how exact they have to be, the bound alone decides.
A program may use at most 64 MiB of HBM per device.

v0:
```python
import functools
import math

import jax
import jax.numpy as jnp
import ml_dtypes
import numpy as np
from jax import lax
from jax.experimental import pallas as pl
from jax.experimental.pallas import tpu as pltpu
from jax.sharding import PartitionSpec as P

PLANE = 512
ZLOC = 2


SCREEN = 0.25
HIGHEST = lax.Precision.HIGHEST
MESH = pl.DeviceIdType.MESH


def swapped(array, axis, distance):
    return lax.ppermute(array, axis, [(i, i ^ 1 << distance) for i in range(lax.axis_size(axis))])


def bit_count(number):
    return number.bit_length() - 1


def reverse_bits(values, digits):
    result = jnp.zeros_like(values)
    for digit in range(digits):
        result = result | (values >> digit & 1) << digits - 1 - digit
    return result


def dft_tables(length, freq_count):
    points = jnp.arange(length, dtype=jnp.int32)[:, None]
    freqs = jnp.arange(freq_count, dtype=jnp.int32)[None, :]
    angles = 2.0 * jnp.pi / length * (points * freqs % length).astype(jnp.float32)
    return (jnp.cos(angles), jnp.sin(angles))


def rotate(values, angles):
    cosine = jnp.cos(angles)
    sine = jnp.sin(angles)
    return (values[0] * cosine + values[1] * sine, values[1] * cosine - values[0] * sine)


def section_angles(z_rows, half, total):
    exponent = z_rows % half * (total // (2 * half))
    return (2.0 * jnp.pi / total * exponent.astype(jnp.float32))[:, None, None]


def combine_pair(mine, theirs, upper, angles):
    summed = (mine[0] + theirs[0], mine[1] + theirs[1])
    turned = rotate((theirs[0] - mine[0], theirs[1] - mine[1]), angles)
    return (jnp.where(upper, turned[0], summed[0]), jnp.where(upper, turned[1], summed[1]))


def local_sections(values, total):
    count = values[0].shape[0]
    shape = values[0].shape
    half = count // 2
    while half >= 1:
        split_real = values[0].reshape((count // (2 * half), 2, half) + shape[1:])
        split_imag = values[1].reshape((count // (2 * half), 2, half) + shape[1:])
        offsets = jnp.arange(half, dtype=jnp.int32) * (total // (2 * half))
        angles = (2.0 * jnp.pi / total * offsets.astype(jnp.float32))[None, :, None, None]
        summed_real = split_real[:, 0] + split_real[:, 1]
        summed_imag = split_imag[:, 0] + split_imag[:, 1]
        turned = rotate(
            (split_real[:, 0] - split_real[:, 1], split_imag[:, 0] - split_imag[:, 1]), angles
        )
        values = (
            jnp.stack([summed_real, turned[0]], axis=1).reshape(shape),
            jnp.stack([summed_imag, turned[1]], axis=1).reshape(shape),
        )
        half = half // 2
    return values


def on_device_wide(brick_data, brick_xy, brick_live):
    layers = brick_live.shape[0]
    capacity = brick_data.shape[0] // layers
    brick = brick_data.shape[1]
    area = brick_data.shape[2]
    zlocal = ZLOC
    per_layer = brick // zlocal
    ngroup = lax.axis_size("zg")
    nplane = lax.axis_size("zl")
    total = zlocal * ngroup * nplane
    width = PLANE
    blocks = width // brick
    kx_count = width // 2 + 1
    group_idx = lax.axis_index("zg")
    plane_idx = lax.axis_index("zl")
    live = (jnp.arange(capacity, dtype=jnp.int32)[None, :] < brick_live).astype(jnp.float32)
    masked = (
        brick_data.reshape(layers, capacity, per_layer, zlocal, area) * live[:, :, None, None, None]
    )
    outgoing = jnp.transpose(masked, (0, 2, 1, 3, 4)).reshape(
        layers * per_layer, capacity, zlocal, area
    )
    block_ids = (
        (brick_xy[1] * blocks + brick_xy[0]).astype(jnp.float32).reshape(layers, 1, capacity)
    )
    block_out = jnp.broadcast_to(block_ids, (layers, per_layer, capacity)).reshape(
        layers * per_layer, capacity
    )
    pieces, places = (
        lax.all_to_all(outgoing, "zl", split_axis=0, concat_axis=0, tiled=True),
        lax.all_to_all(block_out, "zl", split_axis=0, concat_axis=0, tiled=True),
    )
    slot_ids = places.astype(jnp.int32).reshape(-1)
    incoming = jnp.transpose(pieces, (2, 0, 1, 3)).reshape(zlocal, -1, area)
    blockgrid = (
        jnp.zeros((zlocal, blocks * blocks, area), jnp.float32).at[:, slot_ids, :].add(incoming)
    )
    blockgrid = blockgrid.reshape(zlocal, blocks, blocks, brick, brick)
    cos_x, sin_x = dft_tables(width, kx_count)
    cos_x = cos_x.reshape(blocks, brick, kx_count)
    sin_x = sin_x.reshape(blocks, brick, kx_count)
    first_real = jnp.einsum("zabuv,bvk->zkau", blockgrid, cos_x, precision=HIGHEST).reshape(
        zlocal * kx_count, width
    )
    first_imag = -jnp.einsum("zabuv,bvk->zkau", blockgrid, sin_x, precision=HIGHEST).reshape(
        zlocal * kx_count, width
    )
    cos_y, sin_y = dft_tables(width, width)
    second_real = jnp.dot(first_real, cos_y, precision=HIGHEST) + jnp.dot(
        first_imag, sin_y, precision=HIGHEST
    )
    second_imag = jnp.dot(first_imag, cos_y, precision=HIGHEST) - jnp.dot(
        first_real, sin_y, precision=HIGHEST
    )
    values = (
        second_real.reshape(zlocal, kx_count, width),
        second_imag.reshape(zlocal, kx_count, width),
    )
    device = group_idx * nplane + plane_idx
    z_rows = device * zlocal + jnp.arange(zlocal, dtype=jnp.int32)
    gbits = bit_count(ngroup)
    pbits = bit_count(nplane)
    for level in reversed(range(gbits)):
        half = zlocal * nplane * (1 << level)
        theirs = swapped((values[0], values[1]), "zg", level)
        upper = group_idx >> level & 1 == 1
        values = combine_pair(values, theirs, upper, section_angles(z_rows, half, total))
    plane_values = values
    for level in reversed(range(pbits)):
        half = zlocal * (1 << level)
        theirs = swapped((plane_values[0], plane_values[1]), "zl", level)
        upper = plane_idx >> level & 1 == 1
        plane_values = combine_pair(
            plane_values, theirs, upper, section_angles(z_rows, half, total)
        )
    plane_values = local_sections(plane_values, total)
    values = plane_values
    kz_rows = reverse_bits(z_rows, bit_count(total))
    along_z = 4.0 * jnp.sin(jnp.pi * kz_rows.astype(jnp.float32) / total) ** 2
    along_x = 4.0 * jnp.sin(jnp.pi * jnp.arange(kx_count, dtype=jnp.float32) / width) ** 2
    along_y = 4.0 * jnp.sin(jnp.pi * jnp.arange(width, dtype=jnp.float32) / width) ** 2
    denom = along_z[:, None, None] + along_x[None, :, None] + along_y[None, None, :] + SCREEN
    factor = -(1.0 / math.sqrt(width * width * total)) / denom
    return (values[0] * factor, values[1] * factor)


def transposed_blocks(tiles, width):
    tiles = list(tiles)
    block = lax.broadcasted_iota(jnp.int32, tiles[0].shape, tiles[0].ndim - 1) // width
    lanes = tiles[0].shape[-1]
    step = len(tiles) // 2
    while step:
        high = (block & step) != 0
        for i in range(len(tiles)):
            if not i & step:
                low, up = tiles[i], tiles[i + step]
                tiles[i] = jnp.where(high, pltpu.roll(up, step * width, low.ndim - 1), low)
                tiles[i + step] = jnp.where(
                    high, up, pltpu.roll(low, lanes - step * width, low.ndim - 1)
                )
        step //= 2
    return tiles


def exchange_kernel(
    ngroup, nplane, capacity, coef, data, place, out, raw, ready, zsend, zrecv, psend, precv
):
    group, plane = lax.axis_index("zg"), lax.axis_index("zl")
    quads = capacity // 4
    depth = data.shape[0] // quads
    barrier = pltpu.get_barrier_semaphore()

    def greet(g, p):
        pl.semaphore_signal(barrier, inc=1, device_id=(g, p), device_id_type=MESH)

    for k in range(1, nplane):
        greet(group, lax.rem(plane + k, nplane))
    pl.when(group > 0)(lambda: greet(group - 1, plane))
    pl.when(group < ngroup - 1)(lambda: greet(group + 1, plane))
    ends = jnp.where(group > 0, 1, 0) + jnp.where(group < ngroup - 1, 1, 0)
    pl.semaphore_wait(barrier, nplane - 1 + ends)

    def along(side, t):
        chunk = jnp.where(side == 0, group - t, group + t)
        target = jnp.where(side == 0, group + 1, group - 1)
        inside = (chunk >= 0) & (chunk < ngroup) & (target >= 0) & (target < ngroup)
        safe = jnp.clip(chunk, 0, ngroup - 1)
        copy = pltpu.make_async_remote_copy(
            src_ref=raw.at[safe],
            dst_ref=raw.at[safe],
            send_sem=zsend.at[side, t],
            recv_sem=zrecv.at[side, t],
            device_id=(jnp.clip(target, 0, ngroup - 1), plane),
            device_id_type=MESH,
        )
        return inside, copy

    def to_peer(chunk, k):
        return pltpu.make_async_remote_copy(
            src_ref=ready.at[chunk, k],
            dst_ref=out.at[plane, chunk],
            send_sem=psend.at[chunk, k],
            recv_sem=precv.at[chunk, k],
            device_id=(group, lax.rem(plane + k, nplane)),
            device_id_type=MESH,
        )

    def sums(chunk, peer, target):
        row = chunk * nplane + peer
        real = [coef[row, 2 * z] for z in range(depth)]
        imag = [coef[row, 2 * z + 1] for z in range(depth)]
        for quad in range(quads):
            parts = []
            for table in (real, imag):
                for parity in range(2):
                    total = None
                    for z in range(parity, depth, 2):
                        term = raw[chunk, quad * depth + z] * table[z]
                        total = term if total is None else total + term
                    parts.append(total)
            tiles = (parts[0] + parts[1], parts[2] + parts[3], parts[0] - parts[1], parts[2] - parts[3])
            for i, tile in enumerate(transposed_blocks(tiles, 32)):
                target[quad * 4 + i] = tile
        target[capacity] = raw[chunk, quads * depth]

    def share(chunk):
        def one(k, carry):
            sums(chunk, lax.rem(plane + k, nplane), ready.at[chunk, k])
            to_peer(chunk, k).start()
            return carry

        lax.fori_loop(1, nplane, one, 0)
        sums(chunk, plane, out.at[plane, chunk])

    raw[group, : quads * depth] = data[...]
    raw[group, quads * depth] = place[...]
    for side in range(2):
        inside, copy = along(side, 0)
        pl.when(inside)(copy.start)
    share(group)

    def arrival(i, carry):
        t, side = i // 2, lax.rem(i, 2)
        chunk = jnp.where(side == 0, group - 1 - t, group + 1 + t)

        @pl.when((chunk >= 0) & (chunk < ngroup))
        def _():
            safe = jnp.clip(chunk, 0, ngroup - 1)
            pltpu.make_async_remote_copy(
                src_ref=raw.at[safe],
                dst_ref=raw.at[safe],
                send_sem=zsend.at[side, t],
                recv_sem=zrecv.at[side, t],
                device_id=(group, plane),
                device_id_type=MESH,
            ).wait_recv()

            @pl.when(t < ngroup - 2)
            def _():
                inside, copy = along(side, jnp.minimum(t + 1, ngroup - 2))
                pl.when(inside)(copy.start)

            share(safe)

        return carry

    lax.fori_loop(0, 2 * (ngroup - 1), arrival, 0)

    for side in range(2):
        for t in range(ngroup - 1):
            inside, copy = along(side, t)
            pl.when(inside)(copy.wait_send)

    def finish(i, carry):
        copy = to_peer(i // (nplane - 1), 1 + lax.rem(i, nplane - 1))
        copy.wait_send()
        copy.wait_recv()
        return carry

    lax.fori_loop(0, ngroup * (nplane - 1), finish, 0)


def split(values):
    high = values.astype(jnp.bfloat16)
    return high, (values - high.astype(jnp.float32)).astype(jnp.bfloat16)


def dot3(left, right, dims):
    def one(a, b):
        return lax.dot_general(a, b, (dims, ((), ())), preferred_element_type=jnp.float32)

    return one(left[0], right[0]) + (one(left[0], right[1]) + one(left[1], right[0]))


def spectrum_kernel(
    nplane, ngroup, capacity, blocks, evens, scale,
    places, along_z, bricks, tx_even, tx_odd, ty, along_x, along_y, out_real, out_imag, grid, rows, woven,
):
    step = pl.program_id(0)
    half = rows.shape[-1] // 2

    @pl.when(step == 0)
    def _():
        def clear(i, carry):
            grid[pl.ds(i * 32, 32)] = jnp.zeros((32,) + grid.shape[1:], jnp.float32)
            return carry

        lax.fori_loop(0, grid.shape[0] // 32, clear, 0)

        def place(i, carry):
            source, chunk = i // ngroup, lax.rem(i, ngroup)
            ids = [places[i * capacity + c] for c in range(capacity)]
            values = [grid[ids[c]] + bricks[source, chunk, c] for c in range(capacity)]
            for c in range(capacity):
                grid[ids[c]] = values[c]
            return carry

        lax.fori_loop(0, nplane * ngroup, place, 0)

        def arrange(yb, carry):
            for h in range(2):
                first = transposed_blocks([grid[yb * blocks + h * 8 + i] for i in range(8)], 16)
                second = transposed_blocks(
                    [grid[yb * blocks + (h + 2) * 8 + i] for i in range(8)], 16
                )
                for j in range(8):
                    kz, ri, parity = j // 4, j // 2 % 2, j % 2
                    at = (pl.ds(pl.multiple_of(yb * 8, 8), 8), pl.ds(ri * half + h * 128, 128))
                    rows[(0, kz, parity) + at] = first[j] + second[j]
                    rows[(1, kz, parity) + at] = first[j] - second[j]
            return carry

        lax.fori_loop(0, blocks, arrange, 0)

    for odd in range(2):
        table = tx_odd if odd else tx_even
        count = evens[odd]
        padded = table.shape[1] // 2
        products = []
        for parity in range(2):
            field = split(rows[odd, step, parity])
            first = dot3((table[0], table[1]), field, ((1,), (1,)))
            first = jnp.concatenate([first[:padded], first[padded:]], axis=1)
            products.append(dot3(split(first), (ty[parity, 0], ty[parity, 1]), ((1,), (0,))))
        total, rest = products[0] + products[1], products[0] - products[1]
        axis_x = along_x[odd, :padded, :1]
        denom = along_z[step] + axis_x + along_y[...] + SCREEN
        factor = scale / denom
        width = total.shape[1] // 2
        for part, at in ((0, 0), (1, width)):
            value = jnp.concatenate([total[:, at : at + width], rest[:, at : at + width]], axis=1)
            value = value * factor
            for tile in range(value.shape[1] // 128):
                woven[part, tile, pl.ds(odd, count, stride=2), :] = value[
                    :count, tile * 128 : tile * 128 + 128
                ]
    for part, out in ((0, out_real), (1, out_imag)):
        for tile in range(out.shape[2] // 128):
            out[0, :, tile * 128 : tile * 128 + 128] = woven[part, tile, : out.shape[1]]


def parted(table):
    high = table.astype(ml_dtypes.bfloat16)
    low = (table - high.astype(np.float64)).astype(ml_dtypes.bfloat16)
    return np.stack([high, low])


def x_tables(width):
    tables = []
    for odd in range(2):
        count = width // 4 + 1 - odd
        padded = -(-count // 8) * 8
        kx = 2 * np.arange(padded)[:, None] + odd
        angles = 2 * np.pi / width * (kx * np.arange(width // 2)[None, :] % width)
        cosine, sine = np.cos(angles), np.sin(angles)
        tables.append(parted(np.block([[cosine, sine], [-sine, cosine]])))
    return tables


def y_tables(width):
    tables = []
    for parity in range(2):
        y = 2 * np.arange(width // 2)[:, None] + parity
        angles = 2 * np.pi / width * (y * np.arange(width // 2)[None, :] % width)
        cosine, sine = np.cos(angles), np.sin(angles)
        tables.append(parted(np.block([[cosine, -sine], [sine, cosine]])))
    return np.stack(tables)


def kz_of(rows, total):
    digits = bit_count(total)
    return sum((rows >> d & 1) << digits - 1 - d for d in range(digits))


def on_device_once(brick_data, brick_xy, brick_live):
    capacity, brick, area = brick_data.shape
    ngroup, nplane = lax.axis_size("zg"), lax.axis_size("zl")
    total = ZLOC * ngroup * nplane
    width = PLANE
    blocks = width // brick
    group, plane = lax.axis_index("zg"), lax.axis_index("zl")
    quads = capacity // 4

    kz = kz_of(np.arange(total), total).reshape(ngroup, nplane, ZLOC)
    z = np.arange(ngroup * brick).reshape(ngroup, 1, brick)
    angles = 2 * np.pi / total * (kz[:, None, :, None, 0] * z[None] % total)
    coef = np.stack([np.cos(angles), -np.sin(angles)], axis=-1)
    coef = coef.reshape(ngroup, ngroup * nplane, 2 * brick).astype(np.float32)
    coef = lax.dynamic_index_in_dim(jnp.asarray(coef), group, 0, keepdims=False)
    along_z = (4 * np.sin(np.pi * kz / total) ** 2).reshape(-1, ZLOC).astype(np.float32)
    along_z = lax.dynamic_index_in_dim(
        jnp.asarray(along_z), group * nplane + plane, 0, keepdims=False
    )

    live = jnp.arange(capacity, dtype=jnp.int32)[:, None, None] < brick_live[0, 0]
    data = jnp.where(live, brick_data, 0.0).reshape(quads, 4, brick, 8, 32)
    data = jnp.transpose(data, (0, 2, 3, 1, 4)).reshape(quads * brick, 8, 128)
    place = (brick_xy[1] * blocks + brick_xy[0]).astype(jnp.float32)
    place = jnp.pad(place[None, :], ((0, 7), (0, 128 - capacity)))

    vmem = pl.BlockSpec(memory_space=pltpu.VMEM)
    smem = pl.BlockSpec(memory_space=pltpu.SMEM)
    arrived = pl.pallas_call(
        functools.partial(exchange_kernel, ngroup, nplane, capacity),
        out_shape=jax.ShapeDtypeStruct((nplane, ngroup, capacity + 1, 8, 128), jnp.float32),
        in_specs=[smem, vmem, vmem],
        out_specs=vmem,
        scratch_shapes=[
            pltpu.VMEM((ngroup, quads * brick + 1, 8, 128), jnp.float32),
            pltpu.VMEM((ngroup, nplane, capacity + 1, 8, 128), jnp.float32),
            pltpu.SemaphoreType.DMA((2, ngroup - 1)),
            pltpu.SemaphoreType.DMA((2, ngroup - 1)),
            pltpu.SemaphoreType.DMA((ngroup, nplane)),
            pltpu.SemaphoreType.DMA((ngroup, nplane)),
        ],
        compiler_params=pltpu.CompilerParams(
            collective_id=0, has_side_effects=True, vmem_limit_bytes=32 * 2**20
        ),
        name="exchange",
    )(coef, data, place)

    places = arrived[:, :, capacity, 0, :capacity].astype(jnp.int32).reshape(-1)
    tx_even, tx_odd = x_tables(width)
    evens = (width // 4 + 1, width // 4)
    axis = 4 * np.sin(np.pi * np.arange(width) / width) ** 2
    along_x = np.zeros((2, tx_even.shape[1] // 2, 128), np.float32)
    for odd in range(2):
        along_x[odd, : evens[odd]] = axis[odd : width // 2 + 1 : 2][:, None]
    along_y = axis[None, :].astype(np.float32)

    def whole(array):
        return pl.BlockSpec(array.shape, lambda i, n=array.ndim: (0,) * n)

    tables = [jnp.asarray(t) for t in (tx_even, tx_odd, y_tables(width), along_x, along_y)]
    out = jax.ShapeDtypeStruct((ZLOC, width // 2 + 1, width), jnp.float32)
    out_spec = pl.BlockSpec((1, width // 2 + 1, width), lambda i: (i, 0, 0))
    scale = -1.0 / math.sqrt(width * width * total)
    return pl.pallas_call(
        functools.partial(spectrum_kernel, nplane, ngroup, capacity, blocks, evens, scale),
        grid=(ZLOC,),
        out_shape=(out, out),
        in_specs=[smem, smem, whole(arrived)] + [whole(t) for t in tables],
        out_specs=(out_spec, out_spec),
        scratch_shapes=[
            pltpu.VMEM((blocks * blocks, 8, 128), jnp.float32),
            pltpu.VMEM((2, ZLOC, 2, width // 2, width), jnp.float32),
            pltpu.VMEM((2, width // 128, width // 2 + 8, 128), jnp.float32),
        ],
        compiler_params=pltpu.CompilerParams(vmem_limit_bytes=48 * 2**20),
        name="spectrum",
    )(places, along_z, arrived, *tables)


def on_device(brick_data, brick_xy, brick_live):
    layers = brick_live.shape[0]
    slots, brick, area = brick_data.shape
    nplane, ngroup = lax.axis_size("zl"), lax.axis_size("zg")
    one_layer = layers == 1 and nplane * ZLOC == brick and brick == 16 and slots == 16
    fits = slots * nplane * ngroup * area * 2 * ZLOC * 4 <= 4 * 2**20
    if one_layer and fits and ngroup > 1:
        return on_device_once(brick_data, brick_xy, brick_live)
    return on_device_wide(brick_data, brick_xy, brick_live)


def solution(mesh):
    in_specs = (P(("zg", "zl"), None, None), P(None, ("zg", "zl")), P(None, ("zg", "zl")))
    out_specs = (P(("zg", "zl"), None, None), P(("zg", "zl"), None, None))
    return jax.shard_map(
        on_device, mesh=mesh, in_specs=in_specs, out_specs=out_specs, check_vma=False
    )
```

profile of v0, /device:TPU:0, one launch (start us, length us, event | category | flops | bytes accessed | tf_op | source)
XLA Modules:
  0.0 63.7 jit_solution(6277165107634697606)
XLA Ops:
  1.3 0.7 %dynamic-slice_bitcast_fusion.1.along_z = f32[2]{0:T(128)S(1)} fusion(f32[32,2]{1,0:T(8,128)} %constant.41.clone, s32[]{:T(128)S(6)} %select_n.14), kind=kLoop, calls=%fused_computation.4 | loop fusion | bytes 20 | tf_op jit(solution)/shard_map/jit(dynamic_index_in_dim)/squeeze | solution.py:433
  2.0 0.8 %add_convert_fusion = f32[1,16]{1,0:T(1,128)S(1)} fusion(s32[2,16]{1,0:T(2,128)} %param.11), kind=kLoop, calls=%fused_computation.5 | loop fusion | flops 48 | bytes 192 | tf_op jit(solution)/shard_map/convert_element_type | solution.py:440
  2.8 0.7 %dynamic-slice_bitcast_fusion.coef = f32[32,32]{1,0:T(8,128)S(1)} fusion(f32[4,32,32]{2,1,0:T(8,128)} %constant.40.clone, s32[]{:T(128)S(6)} %select_n.12), kind=kLoop, calls=%fused_computation.3 | loop fusion | bytes 8196 | tf_op jit(solution)/shard_map/jit(dynamic_index_in_dim)/squeeze | solution.py:431
  3.5 1.0 %broadcast_select_fusion = f32[16,16,256]{2,1,0:T(8,128)S(1)} fusion(f32[16,16,256]{2,1,0:T(8,128)} %param.10, pred[16]{0:T(512)(128)(4,1)S(1)} %iota_compare_fusion), kind=kLoop, calls=%fused_computation.1 | loop fusion | flops 65536 | bytes 524304 | tf_op jit(solution)/shard_map/jit(_where)/select_n | solution.py:438
  4.5 0.3 reshape.18
  4.8 0.7 %copy.16 = f32[4,4,16,8,32]{4,1,3,2,0:T(4,128)S(1)} copy(f32[4,4,16,8,32]{4,3,2,1,0:T(8,128)S(1)} %reshape.18) | data formatting | bytes 524288 | tf_op jit(solution)/shard_map/reshape | solution.py:438
  5.5 0.5 reshape.19.data
  5.9 0.0 copy-start.2
  6.0 0.0 copy-start.4
  6.0 0.0 copy-start.5
  6.0 34.0 %exchange.1.bricks = f32[8,4,17,8,128]{4,3,2,1,0:T(8,128)S(1)} custom-call(f32[32,32]{1,0:T(8,128)S(1)} %dynamic-slice_bitcast_fusion.coef, f32[64,8,128]{2,1,0:T(8,128)S(1)} %reshape.19.data, f32[8,128]{1,0:T(8,128)S(1)} %pad.4.place), custom_call_target="tpu_custom_call" | custom-call | tf_op jit(solution)/shard_map/exchange/pallas_call | solution.py:445
  40.0 0.0 copy-start
  40.0 0.1 convert_reduce_fusion
  40.1 0.1 convert_element_type.15.places
  40.2 1.2 %copy-done = f32[8,4,17,8,128]{4,3,2,1,0:T(8,128)} copy-done((f32[8,4,17,8,128]{4,3,2,1,0:T(8,128)}, f32[8,4,17,8,128]{4,3,2,1,0:T(8,128)S(1)}, u32[]{:S(2)}) %copy-start) | copy-done | bytes 2228248
  41.4 0.0 copy-done.2
  41.4 0.0 copy-done.4
  41.4 0.0 copy-done.5
  41.4 0.0 copy-start.1
  41.4 1.6 %copy-done.1 = bf16[2,2,512,512]{3,2,1,0:T(8,128)(2,1)S(1)} copy-done((bf16[2,2,512,512]{3,2,1,0:T(8,128)(2,1)S(1)}, bf16[2,2,512,512]{3,2,1,0:T(8,128)(2,1)}, u32[]{:S(2)}) %copy-start.1) | copy-done | bytes 2097176
  43.0 0.0 copy-start.3
  43.0 1.0 %copy-done.3 = bf16[2,256,512]{2,1,0:T(8,128)(2,1)S(1)} copy-done((bf16[2,256,512]{2,1,0:T(8,128)(2,1)S(1)}, bf16[2,256,512]{2,1,0:T(8,128)(2,1)}, u32[]{:S(2)}) %copy-start.3) | copy-done | bytes 524312
  44.0 16.0 %spectrum.1 = (f32[2,257,512]{2,1,0:T(8,128)S(1)}, f32[2,257,512]{2,1,0:T(8,128)S(1)}) custom-call(s32[512]{0:T(512)S(1)} %convert_element_type.15.places, f32[2]{0:T(128)S(1)} %dynamic-slice_bitcast_fusion.1.along_z, f32[8,4,17,8,128]{4,3,2,1,0:T(8,128)} %copy-done, bf16[2,272,512]{2,1,0:T(8,128)(2,1)S(1)} %copy-done.2, bf16[2,256,512]{2,1,0:T(8,128)(2,1)S(1)} %copy-done.3, ...), custom_call_target="tpu_custom_call" | custom-call | tf_op jit(solution)/shard_map/spectrum/pallas_call | solution.py:480
  60.1 1.8 %copy.13 = f32[2,257,512]{2,0,1:T(2,128)} copy(f32[2,257,512]{2,1,0:T(8,128)S(1)} %get-tuple-element.2) | data formatting | bytes 2105344 | tf_op jit(solution)/shard_map/spectrum/pallas_call | solution.py:480
  61.9 1.8 %copy.14 = f32[2,257,512]{2,0,1:T(2,128)} copy(f32[2,257,512]{2,1,0:T(8,128)S(1)} %get-tuple-element.3) | data formatting | bytes 2105344 | tf_op jit(solution)/shard_map/spectrum/pallas_call | solution.py:480
  (2 shorter events, 0.0 us)
Async XLA Ops:
  5.9 35.5 %copy-start.2 = (bf16[2,272,512]{2,1,0:T(8,128)(2,1)S(1)}, bf16[2,272,512]{2,1,0:T(8,128)(2,1)}, u32[]{:S(2)}) copy-start(bf16[2,272,512]{2,1,0:T(8,128)(2,1)} %constant.42.clone.tx_even) | copy-start | bytes 1671172
  6.0 35.5 %copy-start.4 = (f32[2,136,128]{2,1,0:T(8,128)S(1)}, f32[2,136,128]{2,1,0:T(8,128)}, u32[]{:S(2)}) copy-start(f32[2,136,128]{2,1,0:T(8,128)} %constant.45.clone.along_x) | copy-start | bytes 417796
  6.0 35.4 %copy-start.5 = (f32[1,512]{1,0:T(1,128)S(1)}, f32[1,512]{1,0:T(1,128)}, u32[]{:S(2)}) copy-start(f32[1,512]{1,0:T(1,128)} %constant.46.clone.along_y) | copy-start | bytes 6148
  40.0 1.4 %copy-start = (f32[8,4,17,8,128]{4,3,2,1,0:T(8,128)}, f32[8,4,17,8,128]{4,3,2,1,0:T(8,128)S(1)}, u32[]{:S(2)}) copy-start(f32[8,4,17,8,128]{4,3,2,1,0:T(8,128)S(1)} %exchange.1.bricks) | copy-start | bytes 6684676
  41.4 1.6 %copy-start.1 = (bf16[2,2,512,512]{3,2,1,0:T(8,128)(2,1)S(1)}, bf16[2,2,512,512]{3,2,1,0:T(8,128)(2,1)}, u32[]{:S(2)}) copy-start(bf16[2,2,512,512]{3,2,1,0:T(8,128)(2,1)} %constant.44.clone.ty) | copy-start | bytes 6291460
  43.0 1.0 %copy-start.3 = (bf16[2,256,512]{2,1,0:T(8,128)(2,1)S(1)}, bf16[2,256,512]{2,1,0:T(8,128)(2,1)}, u32[]{:S(2)}) copy-start(bf16[2,256,512]{2,1,0:T(8,128)(2,1)} %constant.43.clone.tx_odd) | copy-start | bytes 1572868
where the time goes:
time: 64.2 us; the launch traced here: 63.7 us
  Pallas kernels  50.1 us (78%)
  local copies, waits for them, and re-layouts  10.4 us (16%)
  other arithmetic  1.86 us (3%)
  between operations  1.37 us (2%)
    pallas_call x1, Pallas kernels, on_device_once(): pl.pallas_call(functools.partial(exchange_kernel, ngroup, nplane, capacit...  34 us
    pallas_call x1, Pallas kernels, on_device_once(): pl.pallas_call(functools.partial(spectrum_kernel, nplane, ngroup, capacit...  16 us
    unnamed x12, local copies, waits for them, and re-layouts  3.86 us
    pallas_call x2, local copies, waits for them, and re-layouts, on_device_once(): pl.pallas_call(functools.partial(spectrum_kernel, nplane, ngroup, capacit...  3.57 us

commit v1 on v0

--- a/solution.py
+++ b/solution.py
@@ -166,6 +166,14 @@
     return (values[0] * factor, values[1] * factor)
 
 
+def kz_of(row, total):
+    digits = bit_count(total)
+    return sum(
+        lax.rem(lax.div(row, jnp.int32(1 << d)), jnp.int32(2)) * (1 << digits - 1 - d)
+        for d in range(digits)
+    )
+
+
 def transposed_blocks(tiles, width):
     tiles = list(tiles)
     block = lax.broadcasted_iota(jnp.int32, tiles[0].shape, tiles[0].ndim - 1) // width
@@ -185,11 +193,12 @@
 
 
 def exchange_kernel(
-    ngroup, nplane, capacity, coef, data, place, out, raw, ready, zsend, zrecv, psend, precv
+    ngroup, nplane, capacity, blocks, cosines, live, data, xy, out, raw, ready, zsend, zrecv, psend, precv
 ):
     group, plane = lax.axis_index("zg"), lax.axis_index("zl")
     quads = capacity // 4
-    depth = data.shape[0] // quads
+    depth = data.shape[1]
+    total = cosines.shape[0]
     barrier = pltpu.get_barrier_semaphore()
 
     def greet(g, p):
@@ -228,22 +237,23 @@
         )
 
     def sums(chunk, peer, target):
-        row = chunk * nplane + peer
-        real = [coef[row, 2 * z] for z in range(depth)]
-        imag = [coef[row, 2 * z + 1] for z in range(depth)]
+        kz = kz_of((group * nplane + peer) * ZLOC, total)
+        turns = [lax.rem(kz * (chunk * depth + z), total) for z in range(depth)]
+        real = [cosines[turn] for turn in turns]
+        imag = [cosines[lax.rem(turn + total // 4, total)] for turn in turns]
         for quad in range(quads):
             parts = []
             for table in (real, imag):
                 for parity in range(2):
-                    total = None
+                    summed = None
                     for z in range(parity, depth, 2):
-                        term = raw[chunk, quad * depth + z] * table[z]
-                        total = term if total is None else total + term
-                    parts.append(total)
+                        term = raw[chunk, pl.ds((quad * depth + z) * 8, 8)] * table[z]
+                        summed = term if summed is None else summed + term
+                    parts.append(summed)
             tiles = (parts[0] + parts[1], parts[2] + parts[3], parts[0] - parts[1], parts[2] - parts[3])
             for i, tile in enumerate(transposed_blocks(tiles, 32)):
                 target[quad * 4 + i] = tile
-        target[capacity] = raw[chunk, quads * depth]
+        target[capacity] = raw[chunk, pl.ds(quads * depth * 8, 8)]
 
     def share(chunk):
         def one(k, carry):
@@ -254,8 +264,19 @@
         lax.fori_loop(1, nplane, one, 0)
         sums(chunk, plane, out.at[plane, chunk])
 
-    raw[group, : quads * depth] = data[...]
-    raw[group, quads * depth] = place[...]
+    for quad in range(quads):
+        for z in range(0, depth, 8):
+            for half in range(2):
+                tiles = []
+                for slot in range(quad * 4, quad * 4 + 4):
+                    keep = jnp.where(slot < live[0, 0], 1.0, 0.0)
+                    tiles.append(data[slot, z : z + 8, half * 128 : half * 128 + 128] * keep)
+                for i, tile in enumerate(transposed_blocks(tiles, 32)):
+                    row = (quad * depth + z) * 8 + half * 4 + i
+                    raw[group, pl.ds(row, 8, stride=8), :] = tile
+    place = (xy[1:2, :] * blocks + xy[0:1, :]).astype(jnp.float32)
+    place = jnp.concatenate([place, jnp.zeros((1, 128 - capacity), jnp.float32)], axis=1)
+    raw[group, pl.ds(quads * depth * 8, 8)] = jnp.broadcast_to(place, (8, 128))
     for side in range(2):
         inside, copy = along(side, 0)
         pl.when(inside)(copy.start)
@@ -307,95 +328,99 @@
     return high, (values - high.astype(jnp.float32)).astype(jnp.bfloat16)
 
 
-def dot3(left, right, dims):
-    def one(a, b):
-        return lax.dot_general(a, b, (dims, ((), ())), preferred_element_type=jnp.float32)
-
-    return one(left[0], right[0]) + (one(left[0], right[1]) + one(left[1], right[0]))
-
-
 def spectrum_kernel(
     nplane, ngroup, capacity, blocks, evens, scale,
-    places, along_z, bricks, tx_even, tx_odd, ty, along_x, along_y, out_real, out_imag, grid, rows, woven,
+    places, along_z, bricks, tx_even, tx_odd, ty, along_x, along_y, out_real, out_imag,
+    grid, rows, lines,
 ):
-    step = pl.program_id(0)
     half = rows.shape[-1] // 2
-
-    @pl.when(step == 0)
-    def _():
-        def clear(i, carry):
-            grid[pl.ds(i * 32, 32)] = jnp.zeros((32,) + grid.shape[1:], jnp.float32)
-            return carry
-
-        lax.fori_loop(0, grid.shape[0] // 32, clear, 0)
-
-        def place(i, carry):
-            source, chunk = i // ngroup, lax.rem(i, ngroup)
-            ids = [places[i * capacity + c] for c in range(capacity)]
-            values = [grid[ids[c]] + bricks[source, chunk, c] for c in range(capacity)]
-            for c in range(capacity):
-                grid[ids[c]] = values[c]
-            return carry
-
-        lax.fori_loop(0, nplane * ngroup, place, 0)
-
-        def arrange(yb, carry):
-            for h in range(2):
-                first = transposed_blocks([grid[yb * blocks + h * 8 + i] for i in range(8)], 16)
-                second = transposed_blocks(
-                    [grid[yb * blocks + (h + 2) * 8 + i] for i in range(8)], 16
-                )
-                for j in range(8):
-                    kz, ri, parity = j // 4, j // 2 % 2, j % 2
-                    at = (pl.ds(pl.multiple_of(yb * 8, 8), 8), pl.ds(ri * half + h * 128, 128))
-                    rows[(0, kz, parity) + at] = first[j] + second[j]
-                    rows[(1, kz, parity) + at] = first[j] - second[j]
-            return carry
-
-        lax.fori_loop(0, blocks, arrange, 0)
-
+    width = rows.shape[-1]
+    device = lax.axis_index("zg") * nplane + lax.axis_index("zl")
+    total = along_z.shape[0]
+
+    def clear(i, carry):
+        grid[pl.ds(i * 32, 32)] = jnp.zeros((32,) + grid.shape[1:], jnp.float32)
+        return carry
+
+    lax.fori_loop(0, grid.shape[0] // 32, clear, 0)
+
+    def place(i, carry):
+        source, chunk = i // ngroup, lax.rem(i, ngroup)
+        ids = [places[i * capacity + c] for c in range(capacity)]
+        values = [grid[ids[c]] + bricks[source, chunk, c] for c in range(capacity)]
+        for c in range(capacity):
+            grid[ids[c]] = values[c]
+        return carry
+
+    lax.fori_loop(0, nplane * ngroup, place, 0)
+
+    def arrange(yb, carry):
+        for h in range(2):
+            first = transposed_blocks([grid[yb * blocks + h * 8 + i] for i in range(8)], 16)
+            second = transposed_blocks([grid[yb * blocks + (h + 2) * 8 + i] for i in range(8)], 16)
+            for j in range(8):
+                kz, ri, parity = j // 4, j // 2 % 2, j % 2
+                at = (pl.ds(pl.multiple_of(yb * 8, 8), 8), pl.ds(ri * half + h * 128, 128))
+                rows[(0, kz, parity) + at] = first[j] + second[j]
+                rows[(1, kz, parity) + at] = first[j] - second[j]
+        return carry
+
+    lax.fori_loop(0, blocks, arrange, 0)
+
+    def product(a, b, dims):
+        return lax.dot_general(a, b, (dims, ((), ())), preferred_element_type=jnp.float32)
+
+    padded = along_x.shape[1]
+    for parity in range(2):
+        for odd in range(2):
+            table = tx_odd if odd else tx_even
+            count = table.shape[0] // 2
+            for kz in range(ZLOC):
+                high, low = split(rows[odd, kz, parity])
+                both = product(table[...], high, ((1,), (1,)))
+                first = both[:count] + (both[count:] + product(table[:count], low, ((1,), (1,))))
+                at = pl.ds((odd * ZLOC + kz) * padded, padded)
+                lines[parity, at, :half] = first[:padded]
+                lines[parity, at, half:] = first[padded:]
+
+    results = []
+    for parity in range(2):
+        high, low = split(lines[parity])
+        count = high.shape[0]
+        both = product(jnp.concatenate([high, low], axis=0), ty[parity, 0], ((1,), (0,)))
+        results.append(both[:count] + (both[count:] + product(high, ty[parity, 1], ((1,), (0,)))))
+    lines[0] = results[0] + results[1]
+    lines[1] = results[0] - results[1]
+
+    tiles = width // 128
     for odd in range(2):
-        table = tx_odd if odd else tx_even
-        count = evens[odd]
-        padded = table.shape[1] // 2
-        products = []
-        for parity in range(2):
-            field = split(rows[odd, step, parity])
-            first = dot3((table[0], table[1]), field, ((1,), (1,)))
-            first = jnp.concatenate([first[:padded], first[padded:]], axis=1)
-            products.append(dot3(split(first), (ty[parity, 0], ty[parity, 1]), ((1,), (0,))))
-        total, rest = products[0] + products[1], products[0] - products[1]
-        axis_x = along_x[odd, :padded, :1]
-        denom = along_z[step] + axis_x + along_y[...] + SCREEN
-        factor = scale / denom
-        width = total.shape[1] // 2
-        for part, at in ((0, 0), (1, width)):
-            value = jnp.concatenate([total[:, at : at + width], rest[:, at : at + width]], axis=1)
-            value = value * factor
-            for tile in range(value.shape[1] // 128):
-                woven[part, tile, pl.ds(odd, count, stride=2), :] = value[
-                    :count, tile * 128 : tile * 128 + 128
-                ]
-    for part, out in ((0, out_real), (1, out_imag)):
-        for tile in range(out.shape[2] // 128):
-            out[0, :, tile * 128 : tile * 128 + 128] = woven[part, tile, : out.shape[1]]
+        for kz in range(ZLOC):
+            at = pl.ds((odd * ZLOC + kz) * padded, padded)
+            for tile in range(tiles):
+                lanes = pl.ds(tile * 128, 128)
+                denom = along_z[kz_of(device * ZLOC + kz, total)] + along_x[odd] + along_y[:, lanes] + SCREEN
+                factor = scale / denom
+                sign, lane = tile // (tiles // 2), tile % (tiles // 2) * 128
+                for out, start in ((out_real, 0), (out_imag, half)):
+                    value = lines[sign, at, pl.ds(start + lane, 128)] * factor
+                    row = (odd * tiles + tile) * ZLOC + kz
+                    out[pl.ds(row, evens[odd], stride=2 * tiles * ZLOC), :] = value[: evens[odd]]
 
 
 def parted(table):
     high = table.astype(ml_dtypes.bfloat16)
     low = (table - high.astype(np.float64)).astype(ml_dtypes.bfloat16)
-    return np.stack([high, low])
+    return high, low
 
 
 def x_tables(width):
     tables = []
     for odd in range(2):
-        count = width // 4 + 1 - odd
-        padded = -(-count // 8) * 8
+        padded = -(-(width // 4 + 1) // 8) * 8
         kx = 2 * np.arange(padded)[:, None] + odd
         angles = 2 * np.pi / width * (kx * np.arange(width // 2)[None, :] % width)
         cosine, sine = np.cos(angles), np.sin(angles)
-        tables.append(parted(np.block([[cosine, sine], [-sine, cosine]])))
+        tables.append(np.concatenate(parted(np.block([[cosine, sine], [-sine, cosine]]))))
     return tables
 
 
@@ -405,13 +430,8 @@
         y = 2 * np.arange(width // 2)[:, None] + parity
         angles = 2 * np.pi / width * (y * np.arange(width // 2)[None, :] % width)
         cosine, sine = np.cos(angles), np.sin(angles)
-        tables.append(parted(np.block([[cosine, -sine], [sine, cosine]])))
+        tables.append(np.stack(parted(np.block([[cosine, -sine], [sine, cosine]]))))
     return np.stack(tables)
-
-
-def kz_of(rows, total):
-    digits = bit_count(total)
-    return sum((rows >> d & 1) << digits - 1 - d for d in range(digits))
 
 
 def on_device_once(brick_data, brick_xy, brick_live):
@@ -420,35 +440,20 @@
     total = ZLOC * ngroup * nplane
     width = PLANE
     blocks = width // brick
-    group, plane = lax.axis_index("zg"), lax.axis_index("zl")
     quads = capacity // 4
-
-    kz = kz_of(np.arange(total), total).reshape(ngroup, nplane, ZLOC)
-    z = np.arange(ngroup * brick).reshape(ngroup, 1, brick)
-    angles = 2 * np.pi / total * (kz[:, None, :, None, 0] * z[None] % total)
-    coef = np.stack([np.cos(angles), -np.sin(angles)], axis=-1)
-    coef = coef.reshape(ngroup, ngroup * nplane, 2 * brick).astype(np.float32)
-    coef = lax.dynamic_index_in_dim(jnp.asarray(coef), group, 0, keepdims=False)
-    along_z = (4 * np.sin(np.pi * kz / total) ** 2).reshape(-1, ZLOC).astype(np.float32)
-    along_z = lax.dynamic_index_in_dim(
-        jnp.asarray(along_z), group * nplane + plane, 0, keepdims=False
-    )
-
-    live = jnp.arange(capacity, dtype=jnp.int32)[:, None, None] < brick_live[0, 0]
-    data = jnp.where(live, brick_data, 0.0).reshape(quads, 4, brick, 8, 32)
-    data = jnp.transpose(data, (0, 2, 3, 1, 4)).reshape(quads * brick, 8, 128)
-    place = (brick_xy[1] * blocks + brick_xy[0]).astype(jnp.float32)
-    place = jnp.pad(place[None, :], ((0, 7), (0, 128 - capacity)))
+    turns = np.arange(total) / total
+    cosines = jnp.asarray(np.cos(2 * np.pi * turns).astype(np.float32))
+    along_z = jnp.asarray((4 * np.sin(np.pi * turns) ** 2).astype(np.float32))
 
     vmem = pl.BlockSpec(memory_space=pltpu.VMEM)
     smem = pl.BlockSpec(memory_space=pltpu.SMEM)
     arrived = pl.pallas_call(
-        functools.partial(exchange_kernel, ngroup, nplane, capacity),
+        functools.partial(exchange_kernel, ngroup, nplane, capacity, blocks),
         out_shape=jax.ShapeDtypeStruct((nplane, ngroup, capacity + 1, 8, 128), jnp.float32),
-        in_specs=[smem, vmem, vmem],
+        in_specs=[smem, smem, vmem, vmem],
         out_specs=vmem,
         scratch_shapes=[
-            pltpu.VMEM((ngroup, quads * brick + 1, 8, 128), jnp.float32),
+            pltpu.VMEM((ngroup, (quads * brick + 1) * 8, 128), jnp.float32),
             pltpu.VMEM((ngroup, nplane, capacity + 1, 8, 128), jnp.float32),
             pltpu.SemaphoreType.DMA((2, ngroup - 1)),
             pltpu.SemaphoreType.DMA((2, ngroup - 1)),
@@ -456,41 +461,43 @@
             pltpu.SemaphoreType.DMA((ngroup, nplane)),
         ],
         compiler_params=pltpu.CompilerParams(
-            collective_id=0, has_side_effects=True, vmem_limit_bytes=32 * 2**20
+            collective_id=0, has_side_effects=True, vmem_limit_bytes=12 * 2**20
         ),
         name="exchange",
-    )(coef, data, place)
+    )(cosines, brick_live, brick_data, brick_xy)
 
     places = arrived[:, :, capacity, 0, :capacity].astype(jnp.int32).reshape(-1)
     tx_even, tx_odd = x_tables(width)
     evens = (width // 4 + 1, width // 4)
     axis = 4 * np.sin(np.pi * np.arange(width) / width) ** 2
-    along_x = np.zeros((2, tx_even.shape[1] // 2, 128), np.float32)
+    along_x = np.zeros((2, tx_even.shape[0] // 4, 128), np.float32)
     for odd in range(2):
         along_x[odd, : evens[odd]] = axis[odd : width // 2 + 1 : 2][:, None]
     along_y = axis[None, :].astype(np.float32)
 
-    def whole(array):
-        return pl.BlockSpec(array.shape, lambda i, n=array.ndim: (0,) * n)
-
     tables = [jnp.asarray(t) for t in (tx_even, tx_odd, y_tables(width), along_x, along_y)]
-    out = jax.ShapeDtypeStruct((ZLOC, width // 2 + 1, width), jnp.float32)
-    out_spec = pl.BlockSpec((1, width // 2 + 1, width), lambda i: (i, 0, 0))
+    kx_count = width // 2 + 1
+    out = jax.ShapeDtypeStruct((kx_count * width // 128 * ZLOC, 128), jnp.float32)
     scale = -1.0 / math.sqrt(width * width * total)
-    return pl.pallas_call(
+    results = pl.pallas_call(
         functools.partial(spectrum_kernel, nplane, ngroup, capacity, blocks, evens, scale),
-        grid=(ZLOC,),
         out_shape=(out, out),
-        in_specs=[smem, smem, whole(arrived)] + [whole(t) for t in tables],
-        out_specs=(out_spec, out_spec),
+        in_specs=[smem, smem] + [vmem] * 6,
+        out_specs=(vmem, vmem),
         scratch_shapes=[
             pltpu.VMEM((blocks * blocks, 8, 128), jnp.float32),
             pltpu.VMEM((2, ZLOC, 2, width // 2, width), jnp.float32),
-            pltpu.VMEM((2, width // 128, width // 2 + 8, 128), jnp.float32),
+            pltpu.VMEM((2, 2 * ZLOC * along_x.shape[1], width), jnp.float32),
         ],
-        compiler_params=pltpu.CompilerParams(vmem_limit_bytes=48 * 2**20),
+        compiler_params=pltpu.CompilerParams(vmem_limit_bytes=32 * 2**20),
         name="spectrum",
     )(places, along_z, arrived, *tables)
+
+    def ordered(result):
+        result = result.reshape(kx_count, width // 128, ZLOC, 128)
+        return jnp.transpose(result, (2, 0, 1, 3)).reshape(ZLOC, kx_count, width)
+
+    return tuple(ordered(result) for result in results)
 
 
 def on_device(brick_data, brick_xy, brick_live):

time: 64.2 us -> 55.7 us (0.87)
  local copies, waits for them, and re-layouts: 10.4 us -> 3.98 us
  other arithmetic: 1.86 us -> 0.06 us
    pallas_call x2 -> x0, local copies, waits for them, and re-layouts: 3.57 us -> none  [on_device_once(): pl.pallas_call(functools.partial(spectrum_kernel, nplane, ngroup, capacit...]
    squeeze x2 -> x0, local copies, waits for them, and re-layouts: 1.42 us -> none  [the longest x1 0.72 us: on_device_once(): coef = lax.dynamic_index_in_dim(jnp.asarray(coef), group, 0, keepdims=False)]
    reshape x3 -> x0, local copies, waits for them, and re-layouts: 1.41 us -> none  [the longest x2 0.94 us: on_device_once(): data = jnp.where(live, brick_data, 0.0).reshape(quads, 4, brick, 8, 32)]
    select_n x1 -> x0, other arithmetic: 1.03 us -> none  [on_device_once(): data = jnp.where(live, brick_data, 0.0).reshape(quads, 4, brick, 8, 32)]
    convert_element_type x1 -> x0, other arithmetic: 0.76 us -> none  [on_device_once(): place = (brick_xy[1] * blocks + brick_xy[0]).astype(jnp.float32)]
    unnamed x12 -> x18, local copies, waits for them, and re-layouts: 3.86 us -> 3.89 us
where the time goes in v1:
time: 55.7 us; the launch traced here: 55.4 us
  Pallas kernels  49.9 us (90%)
  local copies, waits for them, and re-layouts  3.98 us (7%)
  between operations  1.44 us (3%)
    pallas_call x1, Pallas kernels, on_device_once(): pl.pallas_call(functools.partial(exchange_kernel, ngroup, nplane, capacit...  34.5 us
    pallas_call x1, Pallas kernels, on_device_once(): pl.pallas_call(functools.partial(spectrum_kernel, nplane, ngroup, capacit...  15.4 us
    unnamed x18, local copies, waits for them, and re-layouts  3.89 us

profile of v1, /device:TPU:0, one launch (start us, length us, event | category | flops | bytes accessed | tf_op | source)
XLA Modules:
  0.0 55.4 jit_solution(2707313822137073710)
XLA Ops:
  0.6 0.0 copy-start.5
  0.6 0.0 copy-start.1
  0.7 0.0 copy-start.2
  1.4 0.0 copy-start.3
  1.4 0.9 %copy-done.3 = f32[16,16,256]{2,1,0:T(8,128)S(1)} copy-done((f32[16,16,256]{2,1,0:T(8,128)S(1)}, f32[16,16,256]{2,1,0:T(8,128)}, u32[]{:S(2)}) %copy-start.3) | copy-done | bytes 262168
  2.4 0.0 copy-start.6
  2.4 0.7 %copy-done.6 = s32[2,16]{1,0:T(2,128)S(1)} copy-done((s32[2,16]{1,0:T(2,128)S(1)}, s32[2,16]{1,0:T(2,128)}, u32[]{:S(2)}) %copy-start.6) | copy-done | bytes 152
  3.0 0.0 copy-start.8
  3.0 0.7 %copy-done.8 = f32[64]{0:T(128)S(1)} copy-done((f32[64]{0:T(128)S(1)}, f32[64]{0:T(128)}, u32[]{:S(2)}) %copy-start.8) | copy-done | bytes 280
  3.7 0.0 copy-start.4
  3.7 0.0 copy-start.7
  3.7 34.5 %exchange.1.bricks = f32[8,4,17,8,128]{4,3,2,1,0:T(8,128)S(1)} custom-call(f32[64]{0:T(128)S(1)} %copy-done.8, s32[1,1]{1,0:T(1,128)S(6)} %copy.14.live, f32[16,16,256]{2,1,0:T(8,128)S(1)} %copy-done.3, s32[2,16]{1,0:T(2,128)S(1)} %copy-done.6), custom_call_target="tpu_custom_call" | custom-call | tf_op jit(solution)/shard_map/exchange/pallas_call | solution.py:450
  38.2 0.1 convert_reduce_fusion
  38.2 0.1 convert_element_type.8.places
  38.3 0.0 copy-done.5
  38.3 0.0 copy-done.1
  38.3 0.0 copy-done.2
  38.3 0.0 copy-done.4
  38.4 0.0 copy-done.7
  38.4 0.0 copy-start
  38.4 1.6 %copy-done = bf16[2,2,512,512]{3,2,1,0:T(8,128)(2,1)S(1)} copy-done((bf16[2,2,512,512]{3,2,1,0:T(8,128)(2,1)S(1)}, bf16[2,2,512,512]{3,2,1,0:T(8,128)(2,1)}, u32[]{:S(2)}) %copy-start) | copy-done | bytes 2097176
  40.0 15.4 %spectrum.1 = (f32[2056,128]{1,0:T(8,128)}, f32[2056,128]{1,0:T(8,128)}) custom-call(s32[512]{0:T(512)S(1)} %convert_element_type.8.places, f32[64]{0:T(128)S(1)} %copy-done.7, f32[8,4,17,8,128]{4,3,2,1,0:T(8,128)S(1)} %exchange.1.bricks, bf16[544,512]{1,0:T(8,128)(2,1)S(1)} %copy-done.2, bf16[544,512]{1,0:T(8,128)(2,1)S(1)} %copy-done.1, ...), custom_call_target="tpu_custom_call" | custom-call | tf_op jit(solution)/shard_map/spectrum/pallas_call | solution.py:482
Async XLA Ops:
  0.6 37.7 %copy-start.5 = (f32[1,512]{1,0:T(1,128)S(1)}, f32[1,512]{1,0:T(1,128)}, u32[]{:S(2)}) copy-start(f32[1,512]{1,0:T(1,128)} %constant.20.clone.along_y) | copy-start | bytes 6148
  0.6 37.7 %copy-start.1 = (bf16[544,512]{1,0:T(8,128)(2,1)S(1)}, bf16[544,512]{1,0:T(8,128)(2,1)}, u32[]{:S(2)}) copy-start(bf16[544,512]{1,0:T(8,128)(2,1)} %constant.17.clone.tx_odd) | copy-start | bytes 1671172
  0.7 37.7 %copy-start.2 = (bf16[544,512]{1,0:T(8,128)(2,1)S(1)}, bf16[544,512]{1,0:T(8,128)(2,1)}, u32[]{:S(2)}) copy-start(bf16[544,512]{1,0:T(8,128)(2,1)} %constant.16.clone.tx_even) | copy-start | bytes 1671172
  1.4 1.0 %copy-start.3 = (f32[16,16,256]{2,1,0:T(8,128)S(1)}, f32[16,16,256]{2,1,0:T(8,128)}, u32[]{:S(2)}) copy-start(f32[16,16,256]{2,1,0:T(8,128)} %data.1) | copy-start | bytes 786436
  2.4 0.7 %copy-start.6 = (s32[2,16]{1,0:T(2,128)S(1)}, s32[2,16]{1,0:T(2,128)}, u32[]{:S(2)}) copy-start(s32[2,16]{1,0:T(2,128)} %xy.1) | copy-start | bytes 388
  3.0 0.7 %copy-start.8 = (f32[64]{0:T(128)S(1)}, f32[64]{0:T(128)}, u32[]{:S(2)}) copy-start(f32[64]{0:T(128)} %constant.14.clone.cosines) | copy-start | bytes 772
  3.7 34.7 %copy-start.4 = (f32[2,136,128]{2,1,0:T(8,128)S(1)}, f32[2,136,128]{2,1,0:T(8,128)}, u32[]{:S(2)}) copy-start(f32[2,136,128]{2,1,0:T(8,128)} %constant.19.clone.along_x) | copy-start | bytes 417796
  3.7 34.7 %copy-start.7 = (f32[64]{0:T(128)S(1)}, f32[64]{0:T(128)}, u32[]{:S(2)}) copy-start(f32[64]{0:T(128)} %constant.15.clone.along_z) | copy-start | bytes 772
  38.4 1.6 %copy-start = (bf16[2,2,512,512]{3,2,1,0:T(8,128)(2,1)S(1)}, bf16[2,2,512,512]{3,2,1,0:T(8,128)(2,1)}, u32[]{:S(2)}) copy-start(bf16[2,2,512,512]{3,2,1,0:T(8,128)(2,1)} %constant.18.clone.ty) | copy-start | bytes 6291460

commit v2 on v1

--- a/solution.py
+++ b/solution.py
@@ -174,6 +174,10 @@
     )
 
 
+def reversed_bits(row, digits):
+    return sum((row >> d & 1) << digits - 1 - d for d in range(digits))
+
+
 def transposed_blocks(tiles, width):
     tiles = list(tiles)
     block = lax.broadcasted_iota(jnp.int32, tiles[0].shape, tiles[0].ndim - 1) // width
@@ -193,12 +197,14 @@
 
 
 def exchange_kernel(
-    ngroup, nplane, capacity, blocks, cosines, live, data, xy, out, raw, ready, zsend, zrecv, psend, precv
+    ngroup, nplane, capacity, blocks,
+    coef, live, bricks, xy, out, data, raw, ready, zsend, zrecv, psend, precv, loaded,
 ):
     group, plane = lax.axis_index("zg"), lax.axis_index("zl")
     quads = capacity // 4
     depth = data.shape[1]
-    total = cosines.shape[0]
+    load = pltpu.make_async_copy(bricks, data, loaded)
+    load.start()
     barrier = pltpu.get_barrier_semaphore()
 
     def greet(g, p):
@@ -237,10 +243,9 @@
         )
 
     def sums(chunk, peer, target):
-        kz = kz_of((group * nplane + peer) * ZLOC, total)
-        turns = [lax.rem(kz * (chunk * depth + z), total) for z in range(depth)]
-        real = [cosines[turn] for turn in turns]
-        imag = [cosines[lax.rem(turn + total // 4, total)] for turn in turns]
+        first = ((group * ngroup + chunk) * nplane + peer) * 2 * depth
+        real = [coef[first + 2 * z] for z in range(depth)]
+        imag = [coef[first + 2 * z + 1] for z in range(depth)]
         for quad in range(quads):
             parts = []
             for table in (real, imag):
@@ -264,6 +269,7 @@
         lax.fori_loop(1, nplane, one, 0)
         sums(chunk, plane, out.at[plane, chunk])
 
+    load.wait()
     for quad in range(quads):
         for z in range(0, depth, 8):
             for half in range(2):
@@ -330,13 +336,20 @@
 
 def spectrum_kernel(
     nplane, ngroup, capacity, blocks, evens, scale,
-    places, along_z, bricks, tx_even, tx_odd, ty, along_x, along_y, out_real, out_imag,
-    grid, rows, lines,
+    places, along_z, bricks, along_x, along_y, tx_hbm, ty_hbm, out_real, out_imag,
+    grid, rows, lines, tx, ty, loaded,
 ):
     half = rows.shape[-1] // 2
     width = rows.shape[-1]
     device = lax.axis_index("zg") * nplane + lax.axis_index("zl")
     total = along_z.shape[0]
+
+    loads = (
+        pltpu.make_async_copy(tx_hbm, tx, loaded.at[0]),
+        pltpu.make_async_copy(ty_hbm, ty, loaded.at[1]),
+    )
+    for load in loads:
+        load.start()
 
     def clear(i, carry):
         grid[pl.ds(i * 32, 32)] = jnp.zeros((32,) + grid.shape[1:], jnp.float32)
@@ -354,18 +367,36 @@
 
     lax.fori_loop(0, nplane * ngroup, place, 0)
 
-    def arrange(yb, carry):
+    batch = 4
+
+    def arrange(step, carry):
         for h in range(2):
-            first = transposed_blocks([grid[yb * blocks + h * 8 + i] for i in range(8)], 16)
-            second = transposed_blocks([grid[yb * blocks + (h + 2) * 8 + i] for i in range(8)], 16)
+            first, second = (
+                transposed_blocks(
+                    [
+                        jnp.stack(
+                            [
+                                grid[(step * batch + n) * blocks + at * 8 + i]
+                                for n in range(batch)
+                            ]
+                        )
+                        for i in range(8)
+                    ],
+                    16,
+                )
+                for at in (h, h + 2)
+            )
             for j in range(8):
                 kz, ri, parity = j // 4, j // 2 % 2, j % 2
-                at = (pl.ds(pl.multiple_of(yb * 8, 8), 8), pl.ds(ri * half + h * 128, 128))
-                rows[(0, kz, parity) + at] = first[j] + second[j]
-                rows[(1, kz, parity) + at] = first[j] - second[j]
+                lanes = pl.ds(ri * half + h * 128, 128)
+                at = pl.ds(pl.multiple_of(step * batch * 8, batch * 8), batch * 8)
+                rows[0, kz, parity, at, lanes] = (first[j] + second[j]).reshape(-1, 128)
+                rows[1, kz, parity, at, lanes] = (first[j] - second[j]).reshape(-1, 128)
         return carry
 
-    lax.fori_loop(0, blocks, arrange, 0)
+    lax.fori_loop(0, blocks // batch, arrange, 0)
+    for load in loads:
+        load.wait()
 
     def product(a, b, dims):
         return lax.dot_general(a, b, (dims, ((), ())), preferred_element_type=jnp.float32)
@@ -373,7 +404,7 @@
     padded = along_x.shape[1]
     for parity in range(2):
         for odd in range(2):
-            table = tx_odd if odd else tx_even
+            table = tx.at[odd]
             count = table.shape[0] // 2
             for kz in range(ZLOC):
                 high, low = split(rows[odd, kz, parity])
@@ -442,54 +473,64 @@
     blocks = width // brick
     quads = capacity // 4
     turns = np.arange(total) / total
-    cosines = jnp.asarray(np.cos(2 * np.pi * turns).astype(np.float32))
+    kz = np.array([reversed_bits(row, bit_count(total)) for row in range(0, total, ZLOC)])
+    angles = kz.reshape(ngroup, 1, nplane, 1) * np.arange(ngroup * brick).reshape(-1, 1, brick)
+    angles = 2 * np.pi / total * (angles % total)
+    coef = np.stack([np.cos(angles), -np.sin(angles)], axis=-1).astype(np.float32).reshape(-1)
     along_z = jnp.asarray((4 * np.sin(np.pi * turns) ** 2).astype(np.float32))
 
     vmem = pl.BlockSpec(memory_space=pltpu.VMEM)
     smem = pl.BlockSpec(memory_space=pltpu.SMEM)
+    hbm = pl.BlockSpec(memory_space=pltpu.HBM)
     arrived = pl.pallas_call(
         functools.partial(exchange_kernel, ngroup, nplane, capacity, blocks),
         out_shape=jax.ShapeDtypeStruct((nplane, ngroup, capacity + 1, 8, 128), jnp.float32),
-        in_specs=[smem, smem, vmem, vmem],
+        in_specs=[smem, smem, hbm, vmem],
         out_specs=vmem,
         scratch_shapes=[
+            pltpu.VMEM(brick_data.shape, jnp.float32),
             pltpu.VMEM((ngroup, (quads * brick + 1) * 8, 128), jnp.float32),
             pltpu.VMEM((ngroup, nplane, capacity + 1, 8, 128), jnp.float32),
             pltpu.SemaphoreType.DMA((2, ngroup - 1)),
             pltpu.SemaphoreType.DMA((2, ngroup - 1)),
             pltpu.SemaphoreType.DMA((ngroup, nplane)),
             pltpu.SemaphoreType.DMA((ngroup, nplane)),
+            pltpu.SemaphoreType.DMA,
         ],
         compiler_params=pltpu.CompilerParams(
-            collective_id=0, has_side_effects=True, vmem_limit_bytes=12 * 2**20
+            collective_id=0, has_side_effects=True, vmem_limit_bytes=60 * 2**20
         ),
         name="exchange",
-    )(cosines, brick_live, brick_data, brick_xy)
+    )(jnp.asarray(coef), brick_live, brick_data, brick_xy)
 
     places = arrived[:, :, capacity, 0, :capacity].astype(jnp.int32).reshape(-1)
-    tx_even, tx_odd = x_tables(width)
+    tx = np.stack(x_tables(width))
     evens = (width // 4 + 1, width // 4)
     axis = 4 * np.sin(np.pi * np.arange(width) / width) ** 2
-    along_x = np.zeros((2, tx_even.shape[0] // 4, 128), np.float32)
+    along_x = np.zeros((2, tx.shape[1] // 4, 128), np.float32)
     for odd in range(2):
         along_x[odd, : evens[odd]] = axis[odd : width // 2 + 1 : 2][:, None]
     along_y = axis[None, :].astype(np.float32)
 
-    tables = [jnp.asarray(t) for t in (tx_even, tx_odd, y_tables(width), along_x, along_y)]
+    ty = y_tables(width)
+    tables = [jnp.asarray(t) for t in (along_x, along_y, tx, ty)]
     kx_count = width // 2 + 1
     out = jax.ShapeDtypeStruct((kx_count * width // 128 * ZLOC, 128), jnp.float32)
     scale = -1.0 / math.sqrt(width * width * total)
     results = pl.pallas_call(
         functools.partial(spectrum_kernel, nplane, ngroup, capacity, blocks, evens, scale),
         out_shape=(out, out),
-        in_specs=[smem, smem] + [vmem] * 6,
+        in_specs=[smem, smem, vmem, vmem, vmem, hbm, hbm],
         out_specs=(vmem, vmem),
         scratch_shapes=[
             pltpu.VMEM((blocks * blocks, 8, 128), jnp.float32),
             pltpu.VMEM((2, ZLOC, 2, width // 2, width), jnp.float32),
             pltpu.VMEM((2, 2 * ZLOC * along_x.shape[1], width), jnp.float32),
+            pltpu.VMEM(tx.shape, tx.dtype),
+            pltpu.VMEM(ty.shape, ty.dtype),
+            pltpu.SemaphoreType.DMA((2,)),
         ],
-        compiler_params=pltpu.CompilerParams(vmem_limit_bytes=32 * 2**20),
+        compiler_params=pltpu.CompilerParams(vmem_limit_bytes=60 * 2**20),
         name="spectrum",
     )(places, along_z, arrived, *tables)
 

time: 55.7 us -> 54.4 us (0.977)
  local copies, waits for them, and re-layouts: 3.98 us -> 0.68 us
  Pallas kernels: 49.9 us -> 51.1 us
  other arithmetic: 0.06 us -> 0.96 us
    unnamed x18 -> x0, local copies, waits for them, and re-layouts: 3.89 us -> none
    pallas_call x1, Pallas kernels: 34.5 us -> 35.8 us  [on_device_once(): pl.pallas_call(functools.partial(exchange_kernel, ngroup, nplane, capacit...]
    convert_element_type x1, other arithmetic: 0.06 us -> 0.96 us  [on_device_once(): places = arrived[:, :, capacity, 0, :capacity].astype(jnp.int32).reshape(-1)]
    convert_element_type x1, local copies, waits for them, and re-layouts: 0.09 us -> 0.68 us  [on_device_once(): places = arrived[:, :, capacity, 0, :capacity].astype(jnp.int32).reshape(-1)]
where the time goes in v2:
time: 54.4 us; the launch traced here: 54 us
  Pallas kernels  51.1 us (94%)
  between operations  1.29 us (2%)
  other arithmetic  0.96 us (2%)
  local copies, waits for them, and re-layouts  0.68 us (1%)
    pallas_call x1, Pallas kernels, on_device_once(): pl.pallas_call(functools.partial(exchange_kernel, ngroup, nplane, capacit...  35.8 us
    pallas_call x1, Pallas kernels, on_device_once(): pl.pallas_call(functools.partial(spectrum_kernel, nplane, ngroup, capacit...  15.3 us

profile of v2, /device:TPU:0, one launch (start us, length us, event | category | flops | bytes accessed | tf_op | source)
XLA Modules:
  0.0 54.0 jit_solution(2814117724770446075)
XLA Ops:
  1.3 35.8 %exchange.1.bricks = f32[8,4,17,8,128]{4,3,2,1,0:T(8,128)} custom-call(f32[4096]{0:T(1024)} %constant.13.clone.coef, s32[1,1]{1,0:T(1,128)S(6)} %copy.13.live, f32[16,16,256]{2,1,0:T(8,128)} %bricks.1, s32[2,16]{1,0:T(2,128)} %xy.1), custom_call_target="tpu_custom_call" | custom-call | tf_op jit(solution)/shard_map/exchange/pallas_call | solution.py:485
  37.1 1.0 %convert_reduce_fusion = s32[8,4,16]{2,1,0:T(4,128)S(1)} fusion(f32[8,4,17,8,128]{4,3,2,1,0:T(8,128)} %exchange.1.bricks), kind=kLoop, calls=%fused_computation | loop fusion | flops 512 | bytes 4096 | tf_op jit(solution)/shard_map/convert_element_type | solution.py:506
  38.1 0.7 %convert_element_type.8.places = s32[512]{0:T(512)} reshape(s32[8,4,16]{2,1,0:T(4,128)S(1)} %convert_reduce_fusion) | data formatting | bytes 4096 | tf_op jit(solution)/shard_map/convert_element_type | solution.py:506
  38.7 15.3 %spectrum.1 = (f32[2056,128]{1,0:T(8,128)}, f32[2056,128]{1,0:T(8,128)}) custom-call(s32[512]{0:T(512)} %convert_element_type.8.places, f32[64]{0:T(128)} %constant.12.clone.along_z, f32[8,4,17,8,128]{4,3,2,1,0:T(8,128)} %exchange.1.bricks, f32[2,136,128]{2,1,0:T(8,128)} %constant.14.clone.along_x, f32[1,512]{1,0:T(1,128)} %constant.15.clone.along_y, ...), custom_call_target="tpu_custom_call" | custom-call | tf_op jit(solution)/shard_map/spectrum/pallas_call | solution.py:520

commit v3 on v2

--- a/solution.py
+++ b/solution.py
@@ -188,6 +188,11 @@
         for i in range(len(tiles)):
             if not i & step:
                 low, up = tiles[i], tiles[i + step]
+                if 2 * step * width == lanes:
+                    swapped_part = pltpu.roll(jnp.where(high, low, up), step * width, low.ndim - 1)
+                    tiles[i] = jnp.where(high, swapped_part, low)
+                    tiles[i + step] = jnp.where(high, up, swapped_part)
+                    continue
                 tiles[i] = jnp.where(high, pltpu.roll(up, step * width, low.ndim - 1), low)
                 tiles[i + step] = jnp.where(
                     high, up, pltpu.roll(low, lanes - step * width, low.ndim - 1)
@@ -198,7 +203,8 @@
 
 def exchange_kernel(
     ngroup, nplane, capacity, blocks,
-    coef, live, bricks, xy, out, data, raw, ready, zsend, zrecv, psend, precv, loaded,
+    coef, live, bricks, xy, out, out_places, data, raw, ready, spots, zsend, zrecv, psend, precv,
+    ssend, srecv, loaded,
 ):
     group, plane = lax.axis_index("zg"), lax.axis_index("zl")
     quads = capacity // 4
@@ -258,7 +264,6 @@
             tiles = (parts[0] + parts[1], parts[2] + parts[3], parts[0] - parts[1], parts[2] - parts[3])
             for i, tile in enumerate(transposed_blocks(tiles, 32)):
                 target[quad * 4 + i] = tile
-        target[capacity] = raw[chunk, pl.ds(quads * depth * 8, 8)]
 
     def share(chunk):
         def one(k, carry):
@@ -315,6 +320,24 @@
 
     lax.fori_loop(0, 2 * (ngroup - 1), arrival, 0)
 
+    spots[...] = jnp.zeros_like(spots)
+    for chunk in range(ngroup):
+        spots[chunk : chunk + 1] = raw[chunk, pl.ds(quads * depth * 8, 1)]
+    out_places[plane] = spots[...]
+
+    def spots_to(k):
+        return pltpu.make_async_remote_copy(
+            src_ref=spots,
+            dst_ref=out_places.at[plane],
+            send_sem=ssend.at[k],
+            recv_sem=srecv.at[k],
+            device_id=(group, lax.rem(plane + k, nplane)),
+            device_id_type=MESH,
+        )
+
+    for k in range(1, nplane):
+        spots_to(k).start()
+
     for side in range(2):
         for t in range(ngroup - 1):
             inside, copy = along(side, t)
@@ -327,6 +350,9 @@
         return carry
 
     lax.fori_loop(0, ngroup * (nplane - 1), finish, 0)
+    for k in range(1, nplane):
+        spots_to(k).wait_send()
+        spots_to(k).wait_recv()
 
 
 def split(values):
@@ -336,21 +362,14 @@
 
 def spectrum_kernel(
     nplane, ngroup, capacity, blocks, evens, scale,
-    places, along_z, bricks, along_x, along_y, tx_hbm, ty_hbm, out_real, out_imag,
-    grid, rows, lines, tx, ty, loaded,
+    places, along_z, bricks, along_x, along_y, tx, ty, out_real, out_imag,
+    grid, rows, lines,
 ):
     half = rows.shape[-1] // 2
     width = rows.shape[-1]
     device = lax.axis_index("zg") * nplane + lax.axis_index("zl")
     total = along_z.shape[0]
 
-    loads = (
-        pltpu.make_async_copy(tx_hbm, tx, loaded.at[0]),
-        pltpu.make_async_copy(ty_hbm, ty, loaded.at[1]),
-    )
-    for load in loads:
-        load.start()
-
     def clear(i, carry):
         grid[pl.ds(i * 32, 32)] = jnp.zeros((32,) + grid.shape[1:], jnp.float32)
         return carry
@@ -358,45 +377,37 @@
     lax.fori_loop(0, grid.shape[0] // 32, clear, 0)
 
     def place(i, carry):
-        source, chunk = i // ngroup, lax.rem(i, ngroup)
-        ids = [places[i * capacity + c] for c in range(capacity)]
-        values = [grid[ids[c]] + bricks[source, chunk, c] for c in range(capacity)]
-        for c in range(capacity):
-            grid[ids[c]] = values[c]
+        chunk, pair = i // (nplane // 2), lax.rem(i, nplane // 2)
+        slots = [(pair * 2 + n, c) for n in range(2) for c in range(capacity)]
+        ids = [places[(source * ngroup + chunk) * capacity + c] for source, c in slots]
+        values = [grid[at] + bricks[source, chunk, c] for at, (source, c) in zip(ids, slots)]
+        for at, value in zip(ids, values):
+            grid[at] = value
         return carry
 
-    lax.fori_loop(0, nplane * ngroup, place, 0)
-
-    batch = 4
+    lax.fori_loop(0, nplane * ngroup // 2, place, 0)
+
+    batch = 2
 
     def arrange(step, carry):
         for h in range(2):
-            first, second = (
-                transposed_blocks(
-                    [
-                        jnp.stack(
-                            [
-                                grid[(step * batch + n) * blocks + at * 8 + i]
-                                for n in range(batch)
-                            ]
-                        )
-                        for i in range(8)
-                    ],
-                    16,
+            tiles = []
+            for i in range(8):
+                first, second = (
+                    jnp.stack([grid[(step * batch + n) * blocks + at + i] for n in range(batch)])
+                    for at in (h * 8, h * 8 + 16)
                 )
-                for at in (h, h + 2)
-            )
-            for j in range(8):
-                kz, ri, parity = j // 4, j // 2 % 2, j % 2
-                lanes = pl.ds(ri * half + h * 128, 128)
-                at = pl.ds(pl.multiple_of(step * batch * 8, batch * 8), batch * 8)
-                rows[0, kz, parity, at, lanes] = (first[j] + second[j]).reshape(-1, 128)
-                rows[1, kz, parity, at, lanes] = (first[j] - second[j]).reshape(-1, 128)
+                tiles.append((first + second, first - second))
+            for side in range(2):
+                lines_of = transposed_blocks([pair[side] for pair in tiles], 16)
+                for j in range(8):
+                    kz, ri, parity = j // 4, j // 2 % 2, j % 2
+                    lanes = pl.ds(ri * half + h * 128, 128)
+                    at = pl.ds(pl.multiple_of(step * batch * 8, batch * 8), batch * 8)
+                    rows[side, kz, parity, at, lanes] = lines_of[j].reshape(-1, 128)
         return carry
 
     lax.fori_loop(0, blocks // batch, arrange, 0)
-    for load in loads:
-        load.wait()
 
     def product(a, b, dims):
         return lax.dot_general(a, b, (dims, ((), ())), preferred_element_type=jnp.float32)
@@ -482,28 +493,37 @@
     vmem = pl.BlockSpec(memory_space=pltpu.VMEM)
     smem = pl.BlockSpec(memory_space=pltpu.SMEM)
     hbm = pl.BlockSpec(memory_space=pltpu.HBM)
-    arrived = pl.pallas_call(
+    arrived, places = pl.pallas_call(
         functools.partial(exchange_kernel, ngroup, nplane, capacity, blocks),
-        out_shape=jax.ShapeDtypeStruct((nplane, ngroup, capacity + 1, 8, 128), jnp.float32),
+        out_shape=(
+            jax.ShapeDtypeStruct((nplane, ngroup, capacity, 8, 128), jnp.float32),
+            jax.ShapeDtypeStruct((nplane, 8, 128), jnp.float32),
+        ),
         in_specs=[smem, smem, hbm, vmem],
-        out_specs=vmem,
+        out_specs=(vmem, vmem),
         scratch_shapes=[
             pltpu.VMEM(brick_data.shape, jnp.float32),
             pltpu.VMEM((ngroup, (quads * brick + 1) * 8, 128), jnp.float32),
-            pltpu.VMEM((ngroup, nplane, capacity + 1, 8, 128), jnp.float32),
+            pltpu.VMEM((ngroup, nplane, capacity, 8, 128), jnp.float32),
+            pltpu.VMEM((8, 128), jnp.float32),
             pltpu.SemaphoreType.DMA((2, ngroup - 1)),
             pltpu.SemaphoreType.DMA((2, ngroup - 1)),
             pltpu.SemaphoreType.DMA((ngroup, nplane)),
             pltpu.SemaphoreType.DMA((ngroup, nplane)),
+            pltpu.SemaphoreType.DMA((nplane,)),
+            pltpu.SemaphoreType.DMA((nplane,)),
             pltpu.SemaphoreType.DMA,
         ],
         compiler_params=pltpu.CompilerParams(
-            collective_id=0, has_side_effects=True, vmem_limit_bytes=60 * 2**20
+            collective_id=0, has_side_effects=True, vmem_limit_bytes=16 * 2**20
+        ),
+        cost_estimate=pl.CostEstimate(
+            flops=0, bytes_accessed=64 * 2**20, transcendentals=0
         ),
         name="exchange",
     )(jnp.asarray(coef), brick_live, brick_data, brick_xy)
 
-    places = arrived[:, :, capacity, 0, :capacity].astype(jnp.int32).reshape(-1)
+    places = places[:, :ngroup, :capacity].astype(jnp.int32).reshape(-1)
     tx = np.stack(x_tables(width))
     evens = (width // 4 + 1, width // 4)
     axis = 4 * np.sin(np.pi * np.arange(width) / width) ** 2
@@ -520,17 +540,14 @@
     results = pl.pallas_call(
         functools.partial(spectrum_kernel, nplane, ngroup, capacity, blocks, evens, scale),
         out_shape=(out, out),
-        in_specs=[smem, smem, vmem, vmem, vmem, hbm, hbm],
+        in_specs=[smem, smem] + [vmem] * 5,
         out_specs=(vmem, vmem),
         scratch_shapes=[
             pltpu.VMEM((blocks * blocks, 8, 128), jnp.float32),
             pltpu.VMEM((2, ZLOC, 2, width // 2, width), jnp.float32),
             pltpu.VMEM((2, 2 * ZLOC * along_x.shape[1], width), jnp.float32),
-            pltpu.VMEM(tx.shape, tx.dtype),
-            pltpu.VMEM(ty.shape, ty.dtype),
-            pltpu.SemaphoreType.DMA((2,)),
         ],
-        compiler_params=pltpu.CompilerParams(vmem_limit_bytes=60 * 2**20),
+        compiler_params=pltpu.CompilerParams(vmem_limit_bytes=32 * 2**20),
         name="spectrum",
     )(places, along_z, arrived, *tables)
 

time: 54.4 us -> 56.7 us (1.042)
  local copies, waits for them, and re-layouts: 0.68 us -> 7.51 us
  Pallas kernels: 51.1 us -> 47.6 us
  other arithmetic: 0.96 us -> 0.01 us
    unnamed x0 -> x16, local copies, waits for them, and re-layouts: none -> 7.42 us
    pallas_call x1, Pallas kernels: 15.3 us -> 12.5 us  [on_device_once(): pl.pallas_call(functools.partial(spectrum_kernel, nplane, ngroup, capacit...]
    convert_element_type x1, other arithmetic: 0.96 us -> 0.01 us  [on_device_once(): places = places[:, :ngroup, :capacity].astype(jnp.int32).reshape(-1)]
    pallas_call x1, Pallas kernels: 35.8 us -> 35.1 us  [on_device_once(): pl.pallas_call(functools.partial(exchange_kernel, ngroup, nplane, capacit...]
    convert_element_type x1 -> x0, local copies, waits for them, and re-layouts: 0.68 us -> none  [on_device_once(): places = arrived[:, :, capacity, 0, :capacity].astype(jnp.int32).reshape(-1)]
where the time goes in v3:
time: 56.7 us; the launch traced here: 56.4 us
  Pallas kernels  47.6 us (84%)
  local copies, waits for them, and re-layouts  7.51 us (13%)
  between operations  1.31 us (2%)
    pallas_call x1, Pallas kernels, on_device_once(): pl.pallas_call(functools.partial(exchange_kernel, ngroup, nplane, capacit...  35.1 us
    pallas_call x1, Pallas kernels, on_device_once(): pl.pallas_call(functools.partial(spectrum_kernel, nplane, ngroup, capacit...  12.5 us
    unnamed x16, local copies, waits for them, and re-layouts  7.42 us

profile of v3, /device:TPU:0, one launch (start us, length us, event | category | flops | bytes accessed | tf_op | source)
XLA Modules:
  0.0 56.4 jit_solution(7294810854589504667)
XLA Ops:
  1.3 0.0 copy-start.2
  1.3 0.9 %copy-done.2 = f32[16,16,256]{2,1,0:T(8,128)S(1)} copy-done((f32[16,16,256]{2,1,0:T(8,128)S(1)}, f32[16,16,256]{2,1,0:T(8,128)}, u32[]{:S(2)}) %copy-start.2) | copy-done | bytes 262168
  2.2 0.0 copy-start.4
  2.2 0.7 %copy-done.4 = f32[4096]{0:T(1024)S(1)} copy-done((f32[4096]{0:T(1024)S(1)}, f32[4096]{0:T(1024)}, u32[]{:S(2)}) %copy-start.4) | copy-done | bytes 16408
  2.9 0.0 copy-start.6
  2.9 0.7 %copy-done.6 = s32[2,16]{1,0:T(2,128)S(1)} copy-done((s32[2,16]{1,0:T(2,128)S(1)}, s32[2,16]{1,0:T(2,128)}, u32[]{:S(2)}) %copy-start.6) | copy-done | bytes 152
  3.6 35.1 %exchange.1 = (f32[8,4,16,8,128]{4,3,2,1,0:T(8,128)S(1)}, f32[8,8,128]{2,1,0:T(8,128)S(1)}) custom-call(f32[4096]{0:T(1024)S(1)} %copy-done.4, s32[1,1]{1,0:T(1,128)S(6)} %copy.13.live, f32[16,16,256]{2,1,0:T(8,128)S(1)} %copy-done.2, s32[2,16]{1,0:T(2,128)S(1)} %copy-done.6), custom_call_target="tpu_custom_call" | custom-call | bytes 67108864 | tf_op jit(solution)/shard_map/exchange/pallas_call | solution.py:496
  38.7 0.1 reshape.19.places
  38.8 0.0 copy-start
  38.8 1.6 %copy-done = bf16[2,2,512,512]{3,2,1,0:T(8,128)(2,1)S(1)} copy-done((bf16[2,2,512,512]{3,2,1,0:T(8,128)(2,1)S(1)}, bf16[2,2,512,512]{3,2,1,0:T(8,128)(2,1)}, u32[]{:S(2)}) %copy-start) | copy-done | bytes 2097176
  40.4 0.0 copy-start.1
  40.4 1.2 %copy-done.1 = bf16[2,544,512]{2,1,0:T(8,128)(2,1)S(1)} copy-done((bf16[2,544,512]{2,1,0:T(8,128)(2,1)S(1)}, bf16[2,544,512]{2,1,0:T(8,128)(2,1)}, u32[]{:S(2)}) %copy-start.1) | copy-done | bytes 1114136
  41.6 0.0 copy-start.3
  41.6 0.9 %copy-done.3 = f32[2,136,128]{2,1,0:T(8,128)S(1)} copy-done((f32[2,136,128]{2,1,0:T(8,128)S(1)}, f32[2,136,128]{2,1,0:T(8,128)}, u32[]{:S(2)}) %copy-start.3) | copy-done | bytes 139288
  42.5 0.0 copy-start.5
  42.5 0.7 %copy-done.5 = f32[1,512]{1,0:T(1,128)S(1)} copy-done((f32[1,512]{1,0:T(1,128)S(1)}, f32[1,512]{1,0:T(1,128)}, u32[]{:S(2)}) %copy-start.5) | copy-done | bytes 2072
  43.2 0.0 copy-start.7
  43.2 0.7 %copy-done.7 = f32[64]{0:T(128)S(1)} copy-done((f32[64]{0:T(128)S(1)}, f32[64]{0:T(128)}, u32[]{:S(2)}) %copy-start.7) | copy-done | bytes 280
  43.9 12.5 %spectrum.1 = (f32[2056,128]{1,0:T(8,128)}, f32[2056,128]{1,0:T(8,128)}) custom-call(s32[512]{0:T(512)S(1)} %reshape.19.places, f32[64]{0:T(128)S(1)} %copy-done.7, f32[8,4,16,8,128]{4,3,2,1,0:T(8,128)S(1)} %get-tuple-element.7.bricks, f32[2,136,128]{2,1,0:T(8,128)S(1)} %copy-done.3, f32[1,512]{1,0:T(1,128)S(1)} %copy-done.5, ...), custom_call_target="tpu_custom_call" | custom-call | tf_op jit(solution)/shard_map/spectrum/pallas_call | solution.py:540
  (1 shorter events, 0.0 us)
Async XLA Ops:
  1.3 1.0 %copy-start.2 = (f32[16,16,256]{2,1,0:T(8,128)S(1)}, f32[16,16,256]{2,1,0:T(8,128)}, u32[]{:S(2)}) copy-start(f32[16,16,256]{2,1,0:T(8,128)} %bricks.1) | copy-start | bytes 786436
  2.2 0.7 %copy-start.4 = (f32[4096]{0:T(1024)S(1)}, f32[4096]{0:T(1024)}, u32[]{:S(2)}) copy-start(f32[4096]{0:T(1024)} %constant.13.clone.coef) | copy-start | bytes 49156
  2.9 0.7 %copy-start.6 = (s32[2,16]{1,0:T(2,128)S(1)}, s32[2,16]{1,0:T(2,128)}, u32[]{:S(2)}) copy-start(s32[2,16]{1,0:T(2,128)} %xy.1) | copy-start | bytes 388
  38.8 1.6 %copy-start = (bf16[2,2,512,512]{3,2,1,0:T(8,128)(2,1)S(1)}, bf16[2,2,512,512]{3,2,1,0:T(8,128)(2,1)}, u32[]{:S(2)}) copy-start(bf16[2,2,512,512]{3,2,1,0:T(8,128)(2,1)} %constant.17.clone.ty) | copy-start | bytes 6291460
  40.4 1.2 %copy-start.1 = (bf16[2,544,512]{2,1,0:T(8,128)(2,1)S(1)}, bf16[2,544,512]{2,1,0:T(8,128)(2,1)}, u32[]{:S(2)}) copy-start(bf16[2,544,512]{2,1,0:T(8,128)(2,1)} %constant.16.clone.tx) | copy-start | bytes 3342340
  41.6 0.9 %copy-start.3 = (f32[2,136,128]{2,1,0:T(8,128)S(1)}, f32[2,136,128]{2,1,0:T(8,128)}, u32[]{:S(2)}) copy-start(f32[2,136,128]{2,1,0:T(8,128)} %constant.14.clone.along_x) | copy-start | bytes 417796
  42.5 0.7 %copy-start.5 = (f32[1,512]{1,0:T(1,128)S(1)}, f32[1,512]{1,0:T(1,128)}, u32[]{:S(2)}) copy-start(f32[1,512]{1,0:T(1,128)} %constant.15.clone.along_y) | copy-start | bytes 6148
  43.2 0.7 %copy-start.7 = (f32[64]{0:T(128)S(1)}, f32[64]{0:T(128)}, u32[]{:S(2)}) copy-start(f32[64]{0:T(128)} %constant.12.clone.along_z) | copy-start | bytes 772

commit v4 on v3

--- a/solution.py
+++ b/solution.py
@@ -248,6 +248,9 @@
             device_id_type=MESH,
         )
 
+    def keep(chunk):
+        return pltpu.make_async_copy(ready.at[chunk, 0], out.at[plane, chunk], psend.at[chunk, 0])
+
     def sums(chunk, peer, target):
         first = ((group * ngroup + chunk) * nplane + peer) * 2 * depth
         real = [coef[first + 2 * z] for z in range(depth)]
@@ -272,7 +275,8 @@
             return carry
 
         lax.fori_loop(1, nplane, one, 0)
-        sums(chunk, plane, out.at[plane, chunk])
+        sums(chunk, plane, ready.at[chunk, 0])
+        keep(chunk).start()
 
     load.wait()
     for quad in range(quads):
@@ -280,8 +284,8 @@
             for half in range(2):
                 tiles = []
                 for slot in range(quad * 4, quad * 4 + 4):
-                    keep = jnp.where(slot < live[0, 0], 1.0, 0.0)
-                    tiles.append(data[slot, z : z + 8, half * 128 : half * 128 + 128] * keep)
+                    alive = jnp.where(slot < live[0, 0], 1.0, 0.0)
+                    tiles.append(data[slot, z : z + 8, half * 128 : half * 128 + 128] * alive)
                 for i, tile in enumerate(transposed_blocks(tiles, 32)):
                     row = (quad * depth + z) * 8 + half * 4 + i
                     raw[group, pl.ds(row, 8, stride=8), :] = tile
@@ -322,8 +326,9 @@
 
     spots[...] = jnp.zeros_like(spots)
     for chunk in range(ngroup):
-        spots[chunk : chunk + 1] = raw[chunk, pl.ds(quads * depth * 8, 1)]
-    out_places[plane] = spots[...]
+        spots[chunk : chunk + 1] = raw[chunk, pl.ds(quads * depth * 8, 1)].astype(jnp.int32)
+    own_spots = pltpu.make_async_copy(spots, out_places.at[plane], ssend.at[0])
+    own_spots.start()
 
     def spots_to(k):
         return pltpu.make_async_remote_copy(
@@ -350,6 +355,9 @@
         return carry
 
     lax.fori_loop(0, ngroup * (nplane - 1), finish, 0)
+    own_spots.wait()
+    for chunk in range(ngroup):
+        keep(chunk).wait()
     for k in range(1, nplane):
         spots_to(k).wait_send()
         spots_to(k).wait_recv()
@@ -361,14 +369,24 @@
 
 
 def spectrum_kernel(
-    nplane, ngroup, capacity, blocks, evens, scale,
-    places, along_z, bricks, along_x, along_y, tx, ty, out_real, out_imag,
-    grid, rows, lines,
+    nplane, ngroup, capacity, blocks, evens, total, scale,
+    places_hbm, bricks_hbm, tx_hbm, ty_hbm, out_real, out_imag,
+    grid, rows, lines, places, bricks, tx, ty, loaded,
 ):
     half = rows.shape[-1] // 2
     width = rows.shape[-1]
     device = lax.axis_index("zg") * nplane + lax.axis_index("zl")
-    total = along_z.shape[0]
+    loads = [pltpu.make_async_copy(places_hbm, places, loaded.at[0])]
+    for chunk in range(ngroup):
+        loads.append(
+            pltpu.make_async_copy(
+                bricks_hbm.at[:, chunk], bricks.at[:, chunk], loaded.at[1 + chunk]
+            )
+        )
+    loads.append(pltpu.make_async_copy(tx_hbm, tx, loaded.at[1 + ngroup]))
+    loads.append(pltpu.make_async_copy(ty_hbm, ty, loaded.at[2 + ngroup]))
+    for load in loads:
+        load.start()
 
     def clear(i, carry):
         grid[pl.ds(i * 32, 32)] = jnp.zeros((32,) + grid.shape[1:], jnp.float32)
@@ -376,16 +394,17 @@
 
     lax.fori_loop(0, grid.shape[0] // 32, clear, 0)
 
-    def place(i, carry):
-        chunk, pair = i // (nplane // 2), lax.rem(i, nplane // 2)
+    def place(chunk, pair):
         slots = [(pair * 2 + n, c) for n in range(2) for c in range(capacity)]
-        ids = [places[(source * ngroup + chunk) * capacity + c] for source, c in slots]
+        ids = [places[source, chunk, c] for source, c in slots]
         values = [grid[at] + bricks[source, chunk, c] for at, (source, c) in zip(ids, slots)]
         for at, value in zip(ids, values):
             grid[at] = value
-        return carry
-
-    lax.fori_loop(0, nplane * ngroup // 2, place, 0)
+
+    loads[0].wait()
+    for chunk in range(ngroup):
+        loads[1 + chunk].wait()
+        lax.fori_loop(0, nplane // 2, lambda pair, carry: (place(chunk, pair), carry)[1], 0)
 
     batch = 2
 
@@ -408,11 +427,12 @@
         return carry
 
     lax.fori_loop(0, blocks // batch, arrange, 0)
+    loads[1 + ngroup].wait()
 
     def product(a, b, dims):
         return lax.dot_general(a, b, (dims, ((), ())), preferred_element_type=jnp.float32)
 
-    padded = along_x.shape[1]
+    padded = tx.shape[1] // 4
     for parity in range(2):
         for odd in range(2):
             table = tx.at[odd]
@@ -425,6 +445,7 @@
                 lines[parity, at, :half] = first[:padded]
                 lines[parity, at, half:] = first[padded:]
 
+    loads[2 + ngroup].wait()
     results = []
     for parity in range(2):
         high, low = split(lines[parity])
@@ -434,13 +455,20 @@
     lines[0] = results[0] + results[1]
     lines[1] = results[0] - results[1]
 
+    def along(index, count):
+        return 4.0 * jnp.sin(jnp.pi * index.astype(jnp.float32) / count) ** 2
+
     tiles = width // 128
     for odd in range(2):
+        down = lax.broadcasted_iota(jnp.int32, (padded, 1), 0) * 2 + odd
+        along_x = jnp.broadcast_to(along(down, width), (padded, 128))
         for kz in range(ZLOC):
+            turn = jnp.full((8, 128), kz_of(device * ZLOC + kz, total), jnp.int32)
+            along_z = along(turn, total)[:1]
             at = pl.ds((odd * ZLOC + kz) * padded, padded)
             for tile in range(tiles):
-                lanes = pl.ds(tile * 128, 128)
-                denom = along_z[kz_of(device * ZLOC + kz, total)] + along_x[odd] + along_y[:, lanes] + SCREEN
+                across = lax.broadcasted_iota(jnp.int32, (8, 128), 1) + tile * 128
+                denom = along_z + along_x + along(across, width)[:1] + SCREEN
                 factor = scale / denom
                 sign, lane = tile // (tiles // 2), tile % (tiles // 2) * 128
                 for out, start in ((out_real, 0), (out_imag, half)):
@@ -483,29 +511,27 @@
     width = PLANE
     blocks = width // brick
     quads = capacity // 4
-    turns = np.arange(total) / total
     kz = np.array([reversed_bits(row, bit_count(total)) for row in range(0, total, ZLOC)])
     angles = kz.reshape(ngroup, 1, nplane, 1) * np.arange(ngroup * brick).reshape(-1, 1, brick)
     angles = 2 * np.pi / total * (angles % total)
     coef = np.stack([np.cos(angles), -np.sin(angles)], axis=-1).astype(np.float32).reshape(-1)
-    along_z = jnp.asarray((4 * np.sin(np.pi * turns) ** 2).astype(np.float32))
 
     vmem = pl.BlockSpec(memory_space=pltpu.VMEM)
     smem = pl.BlockSpec(memory_space=pltpu.SMEM)
-    hbm = pl.BlockSpec(memory_space=pltpu.HBM)
+    anywhere = pl.BlockSpec(memory_space=pl.ANY)
     arrived, places = pl.pallas_call(
         functools.partial(exchange_kernel, ngroup, nplane, capacity, blocks),
         out_shape=(
             jax.ShapeDtypeStruct((nplane, ngroup, capacity, 8, 128), jnp.float32),
-            jax.ShapeDtypeStruct((nplane, 8, 128), jnp.float32),
+            jax.ShapeDtypeStruct((nplane, 8, 128), jnp.int32),
         ),
-        in_specs=[smem, smem, hbm, vmem],
-        out_specs=(vmem, vmem),
+        in_specs=[smem, smem, anywhere, vmem],
+        out_specs=(anywhere, anywhere),
         scratch_shapes=[
             pltpu.VMEM(brick_data.shape, jnp.float32),
             pltpu.VMEM((ngroup, (quads * brick + 1) * 8, 128), jnp.float32),
             pltpu.VMEM((ngroup, nplane, capacity, 8, 128), jnp.float32),
-            pltpu.VMEM((8, 128), jnp.float32),
+            pltpu.VMEM((8, 128), jnp.int32),
             pltpu.SemaphoreType.DMA((2, ngroup - 1)),
             pltpu.SemaphoreType.DMA((2, ngroup - 1)),
             pltpu.SemaphoreType.DMA((ngroup, nplane)),
@@ -515,41 +541,35 @@
             pltpu.SemaphoreType.DMA,
         ],
         compiler_params=pltpu.CompilerParams(
-            collective_id=0, has_side_effects=True, vmem_limit_bytes=16 * 2**20
-        ),
-        cost_estimate=pl.CostEstimate(
-            flops=0, bytes_accessed=64 * 2**20, transcendentals=0
+            collective_id=0, has_side_effects=True, vmem_limit_bytes=60 * 2**20
         ),
         name="exchange",
     )(jnp.asarray(coef), brick_live, brick_data, brick_xy)
 
-    places = places[:, :ngroup, :capacity].astype(jnp.int32).reshape(-1)
     tx = np.stack(x_tables(width))
     evens = (width // 4 + 1, width // 4)
-    axis = 4 * np.sin(np.pi * np.arange(width) / width) ** 2
-    along_x = np.zeros((2, tx.shape[1] // 4, 128), np.float32)
-    for odd in range(2):
-        along_x[odd, : evens[odd]] = axis[odd : width // 2 + 1 : 2][:, None]
-    along_y = axis[None, :].astype(np.float32)
-
     ty = y_tables(width)
-    tables = [jnp.asarray(t) for t in (along_x, along_y, tx, ty)]
     kx_count = width // 2 + 1
     out = jax.ShapeDtypeStruct((kx_count * width // 128 * ZLOC, 128), jnp.float32)
     scale = -1.0 / math.sqrt(width * width * total)
     results = pl.pallas_call(
-        functools.partial(spectrum_kernel, nplane, ngroup, capacity, blocks, evens, scale),
+        functools.partial(spectrum_kernel, nplane, ngroup, capacity, blocks, evens, total, scale),
         out_shape=(out, out),
-        in_specs=[smem, smem] + [vmem] * 5,
+        in_specs=[anywhere] * 4,
         out_specs=(vmem, vmem),
         scratch_shapes=[
             pltpu.VMEM((blocks * blocks, 8, 128), jnp.float32),
             pltpu.VMEM((2, ZLOC, 2, width // 2, width), jnp.float32),
-            pltpu.VMEM((2, 2 * ZLOC * along_x.shape[1], width), jnp.float32),
+            pltpu.VMEM((2, ZLOC * tx.shape[1] // 2, width), jnp.float32),
+            pltpu.SMEM(places.shape, jnp.int32),
+            pltpu.VMEM(arrived.shape, jnp.float32),
+            pltpu.VMEM(tx.shape, tx.dtype),
+            pltpu.VMEM(ty.shape, ty.dtype),
+            pltpu.SemaphoreType.DMA((3 + ngroup,)),
         ],
-        compiler_params=pltpu.CompilerParams(vmem_limit_bytes=32 * 2**20),
+        compiler_params=pltpu.CompilerParams(vmem_limit_bytes=60 * 2**20),
         name="spectrum",
-    )(places, along_z, arrived, *tables)
+    )(places, arrived, jnp.asarray(tx), jnp.asarray(ty))
 
     def ordered(result):
         result = result.reshape(kx_count, width // 128, ZLOC, 128)

time: 56.7 us -> 50.5 us (0.89)
  local copies, waits for them, and re-layouts: 7.51 us -> 0 us
  Pallas kernels: 47.6 us -> 49 us
    unnamed x16 -> x0, local copies, waits for them, and re-layouts: 7.42 us -> none
    pallas_call x1, Pallas kernels: 35.1 us -> 35.8 us  [on_device_once(): pl.pallas_call(functools.partial(exchange_kernel, ngroup, nplane, capacit...]
    pallas_call x1, Pallas kernels: 12.5 us -> 13.2 us  [on_device_once(): pl.pallas_call(functools.partial(spectrum_kernel, nplane, ngroup, capacit...]
where the time goes in v4:
time: 50.5 us; the launch traced here: 50.3 us
  Pallas kernels  49 us (97%)
  between operations  1.28 us (3%)
    pallas_call x1, Pallas kernels, on_device_once(): pl.pallas_call(functools.partial(exchange_kernel, ngroup, nplane, capacit...  35.8 us
    pallas_call x1, Pallas kernels, on_device_once(): pl.pallas_call(functools.partial(spectrum_kernel, nplane, ngroup, capacit...  13.2 us

profile of v4, /device:TPU:0, one launch (start us, length us, event | category | flops | bytes accessed | tf_op | source)
XLA Modules:
  0.0 50.3 jit_solution(16430814675777744098)
XLA Ops:
  1.3 35.8 %exchange.1 = (f32[8,4,16,8,128]{4,3,2,1,0:T(8,128)}, s32[8,8,128]{2,1,0:T(8,128)}) custom-call(f32[4096]{0:T(1024)} %constant.6.clone.coef, s32[1,1]{1,0:T(1,128)S(6)} %copy.10.live, f32[16,16,256]{2,1,0:T(8,128)} %bricks.1, s32[2,16]{1,0:T(2,128)} %xy.1), custom_call_target="tpu_custom_call" | custom-call | tf_op jit(solution)/shard_map/exchange/pallas_call | solution.py:522
  37.1 13.2 %spectrum.1 = (f32[2056,128]{1,0:T(8,128)}, f32[2056,128]{1,0:T(8,128)}) custom-call(s32[8,8,128]{2,1,0:T(8,128)} %get-tuple-element.6.places_hbm, f32[8,4,16,8,128]{4,3,2,1,0:T(8,128)} %get-tuple-element.7.bricks_hbm, bf16[2,544,512]{2,1,0:T(8,128)(2,1)} %constant.7.clone.tx_hbm, bf16[2,2,512,512]{3,2,1,0:T(8,128)(2,1)} %constant.8.clone.ty_hbm), custom_call_target="tpu_custom_call" | custom-call | tf_op jit(solution)/shard_map/spectrum/pallas_call | solution.py:555

commit v5 on v4

--- a/solution.py
+++ b/solution.py
@@ -348,20 +348,32 @@
             inside, copy = along(side, t)
             pl.when(inside)(copy.wait_send)
 
-    def finish(i, carry):
-        copy = to_peer(i // (nplane - 1), 1 + lax.rem(i, nplane - 1))
-        copy.wait_send()
-        copy.wait_recv()
-        return carry
-
-    lax.fori_loop(0, ngroup * (nplane - 1), finish, 0)
     own_spots.wait()
-    for chunk in range(ngroup):
-        keep(chunk).wait()
     for k in range(1, nplane):
         spots_to(k).wait_send()
         spots_to(k).wait_recv()
 
+    def finish(chunk):
+        keep(chunk).wait()
+
+        def one(k, carry):
+            copy = to_peer(chunk, k)
+            copy.wait_send()
+            copy.wait_recv()
+            return carry
+
+        lax.fori_loop(1, nplane, one, 0)
+
+    finish(group)
+
+    def farther(i, carry):
+        t, side = i // 2, lax.rem(i, 2)
+        chunk = jnp.where(side == 0, group - 1 - t, group + 1 + t)
+        pl.when((chunk >= 0) & (chunk < ngroup))(lambda: finish(jnp.clip(chunk, 0, ngroup - 1)))
+        return carry
+
+    lax.fori_loop(0, 2 * (ngroup - 1), farther, 0)
+
 
 def split(values):
     high = values.astype(jnp.bfloat16)
@@ -370,8 +382,8 @@
 
 def spectrum_kernel(
     nplane, ngroup, capacity, blocks, evens, total, scale,
-    places_hbm, bricks_hbm, tx_hbm, ty_hbm, out_real, out_imag,
-    grid, rows, lines, places, bricks, tx, ty, loaded,
+    places_hbm, bricks_hbm, tx_hbm, ty_hbm, real_hbm, imag_hbm,
+    grid, rows, lines, places, bricks, tx, ty, out_real, out_imag, loaded, stored,
 ):
     half = rows.shape[-1] // 2
     width = rows.shape[-1]
@@ -459,22 +471,37 @@
         return 4.0 * jnp.sin(jnp.pi * index.astype(jnp.float32) / count) ** 2
 
     tiles = width // 128
-    for odd in range(2):
-        down = lax.broadcasted_iota(jnp.int32, (padded, 1), 0) * 2 + odd
-        along_x = jnp.broadcast_to(along(down, width), (padded, 128))
-        for kz in range(ZLOC):
-            turn = jnp.full((8, 128), kz_of(device * ZLOC + kz, total), jnp.int32)
-            along_z = along(turn, total)[:1]
-            at = pl.ds((odd * ZLOC + kz) * padded, padded)
-            for tile in range(tiles):
-                across = lax.broadcasted_iota(jnp.int32, (8, 128), 1) + tile * 128
-                denom = along_z + along_x + along(across, width)[:1] + SCREEN
-                factor = scale / denom
-                sign, lane = tile // (tiles // 2), tile % (tiles // 2) * 128
-                for out, start in ((out_real, 0), (out_imag, half)):
-                    value = lines[sign, at, pl.ds(start + lane, 128)] * factor
-                    row = (odd * tiles + tile) * ZLOC + kz
-                    out[pl.ds(row, evens[odd], stride=2 * tiles * ZLOC), :] = value[: evens[odd]]
+    line = tiles * ZLOC
+    stores = []
+    for low, high in ((0, evens[1] // 2), (evens[1] // 2, padded)):
+        for odd in range(2):
+            count = min(high, evens[odd]) - low
+            index = lax.broadcasted_iota(jnp.int32, (high - low, 1), 0) + low
+            along_x = jnp.broadcast_to(along(index * 2 + odd, width), (high - low, 128))
+            for kz in range(ZLOC):
+                turn = jnp.full((8, 128), kz_of(device * ZLOC + kz, total), jnp.int32)
+                along_z = along(turn, total)[:1]
+                at = pl.ds((odd * ZLOC + kz) * padded + low, high - low)
+                for tile in range(tiles):
+                    across = lax.broadcasted_iota(jnp.int32, (8, 128), 1) + tile * 128
+                    denom = along_z + along_x + along(across, width)[:1] + SCREEN
+                    factor = scale / denom
+                    sign, lane = tile // (tiles // 2), tile % (tiles // 2) * 128
+                    for out, start in ((out_real, 0), (out_imag, half)):
+                        value = lines[sign, at, pl.ds(start + lane, 128)] * factor
+                        row = (low * 2 + odd) * line + tile * ZLOC + kz
+                        out[pl.ds(row, count, stride=2 * line), :] = value[:count]
+        first, last = low * 2 * line, min(high * 2 * line, out_real.shape[0])
+        for i, (source, target) in enumerate(((out_real, real_hbm), (out_imag, imag_hbm))):
+            span = pl.ds(first, last - first)
+            stores.append(
+                pltpu.make_async_copy(
+                    source.at[span], target.at[span], stored.at[len(stores)]
+                )
+            )
+            stores[-1].start()
+    for store in stores:
+        store.wait()
 
 
 def parted(table):
@@ -556,7 +583,7 @@
         functools.partial(spectrum_kernel, nplane, ngroup, capacity, blocks, evens, total, scale),
         out_shape=(out, out),
         in_specs=[anywhere] * 4,
-        out_specs=(vmem, vmem),
+        out_specs=(anywhere, anywhere),
         scratch_shapes=[
             pltpu.VMEM((blocks * blocks, 8, 128), jnp.float32),
             pltpu.VMEM((2, ZLOC, 2, width // 2, width), jnp.float32),
@@ -565,7 +592,10 @@
             pltpu.VMEM(arrived.shape, jnp.float32),
             pltpu.VMEM(tx.shape, tx.dtype),
             pltpu.VMEM(ty.shape, ty.dtype),
+            pltpu.VMEM(out.shape, jnp.float32),
+            pltpu.VMEM(out.shape, jnp.float32),
             pltpu.SemaphoreType.DMA((3 + ngroup,)),
+            pltpu.SemaphoreType.DMA((4,)),
         ],
         compiler_params=pltpu.CompilerParams(vmem_limit_bytes=60 * 2**20),
         name="spectrum",

time: 50.5 us -> 50.8 us (level)
  no operation moved by 1% of the time
where the time goes in v5:
time: 50.8 us; the launch traced here: 50.5 us
  Pallas kernels  49.2 us (97%)
  between operations  1.28 us (3%)
    pallas_call x1, Pallas kernels, on_device_once(): pl.pallas_call(functools.partial(exchange_kernel, ngroup, nplane, capacit...  36.2 us
    pallas_call x1, Pallas kernels, on_device_once(): pl.pallas_call(functools.partial(spectrum_kernel, nplane, ngroup, capacit...  13.1 us

profile of v5, /device:TPU:0, one launch (start us, length us, event | category | flops | bytes accessed | tf_op | source)
XLA Modules:
  0.0 50.5 jit_solution(5224720518805043303)
XLA Ops:
  1.3 36.2 %exchange.1 = (f32[8,4,16,8,128]{4,3,2,1,0:T(8,128)}, s32[8,8,128]{2,1,0:T(8,128)}) custom-call(f32[4096]{0:T(1024)} %constant.6.clone.coef, s32[1,1]{1,0:T(1,128)S(6)} %copy.10.live, f32[16,16,256]{2,1,0:T(8,128)} %bricks.1, s32[2,16]{1,0:T(2,128)} %xy.1), custom_call_target="tpu_custom_call" | custom-call | tf_op jit(solution)/shard_map/exchange/pallas_call | solution.py:549
  37.4 13.1 %spectrum.1 = (f32[2056,128]{1,0:T(8,128)}, f32[2056,128]{1,0:T(8,128)}) custom-call(s32[8,8,128]{2,1,0:T(8,128)} %get-tuple-element.6.places_hbm, f32[8,4,16,8,128]{4,3,2,1,0:T(8,128)} %get-tuple-element.7.bricks_hbm, bf16[2,544,512]{2,1,0:T(8,128)(2,1)} %constant.7.clone.tx_hbm, bf16[2,2,512,512]{3,2,1,0:T(8,128)(2,1)} %constant.8.clone.ty_hbm), custom_call_target="tpu_custom_call" | custom-call | tf_op jit(solution)/shard_map/spectrum/pallas_call | solution.py:582

commit v6 on v5

--- a/solution.py
+++ b/solution.py
@@ -203,8 +203,8 @@
 
 def exchange_kernel(
     ngroup, nplane, capacity, blocks,
-    coef, live, bricks, xy, out, out_places, data, raw, ready, spots, zsend, zrecv, psend, precv,
-    ssend, srecv, loaded,
+    coef, live, bricks, xy, out, out_places, data, raw, ready, mine, theirs, spots, zsend, zrecv, psend, precv,
+    ssend, srecv, lsend, lrecv, loaded,
 ):
     group, plane = lax.axis_index("zg"), lax.axis_index("zl")
     quads = capacity // 4
@@ -218,10 +218,9 @@
 
     for k in range(1, nplane):
         greet(group, lax.rem(plane + k, nplane))
-    pl.when(group > 0)(lambda: greet(group - 1, plane))
-    pl.when(group < ngroup - 1)(lambda: greet(group + 1, plane))
-    ends = jnp.where(group > 0, 1, 0) + jnp.where(group < ngroup - 1, 1, 0)
-    pl.semaphore_wait(barrier, nplane - 1 + ends)
+    for k in range(1, ngroup):
+        greet(lax.rem(group + k, ngroup), plane)
+    pl.semaphore_wait(barrier, nplane - 1 + ngroup - 1)
 
     def along(side, t):
         chunk = jnp.where(side == 0, group - t, group + t)
@@ -278,6 +277,22 @@
         sums(chunk, plane, ready.at[chunk, 0])
         keep(chunk).start()
 
+    place = xy[1:2, :] * blocks + xy[0:1, :]
+    place = jnp.concatenate([place, jnp.zeros((1, 128 - capacity), jnp.int32)], axis=1)
+    mine[...] = jnp.broadcast_to(place, mine.shape)
+
+    def line_to(k):
+        return pltpu.make_async_remote_copy(
+            src_ref=mine,
+            dst_ref=theirs.at[k],
+            send_sem=lsend.at[k],
+            recv_sem=lrecv.at[k],
+            device_id=(lax.rem(group + k, ngroup), plane),
+            device_id_type=MESH,
+        )
+
+    for k in range(1, ngroup):
+        line_to(k).start()
     load.wait()
     for quad in range(quads):
         for z in range(0, depth, 8):
@@ -289,13 +304,33 @@
                 for i, tile in enumerate(transposed_blocks(tiles, 32)):
                     row = (quad * depth + z) * 8 + half * 4 + i
                     raw[group, pl.ds(row, 8, stride=8), :] = tile
-    place = (xy[1:2, :] * blocks + xy[0:1, :]).astype(jnp.float32)
-    place = jnp.concatenate([place, jnp.zeros((1, 128 - capacity), jnp.float32)], axis=1)
-    raw[group, pl.ds(quads * depth * 8, 8)] = jnp.broadcast_to(place, (8, 128))
     for side in range(2):
         inside, copy = along(side, 0)
         pl.when(inside)(copy.start)
     share(group)
+    line = [line_to(k) for k in range(1, ngroup)]
+    for copy in line:
+        copy.wait_recv()
+    spots[...] = jnp.zeros_like(spots)
+    spots[pl.ds(group, 1)] = mine[:1]
+    for k in range(1, ngroup):
+        source = lax.rem(group + ngroup - k, ngroup)
+        spots[pl.ds(source, 1)] = theirs[k, :1]
+    own_spots = pltpu.make_async_copy(spots, out_places.at[plane], ssend.at[0])
+    own_spots.start()
+
+    def spots_to(k):
+        return pltpu.make_async_remote_copy(
+            src_ref=spots,
+            dst_ref=out_places.at[plane],
+            send_sem=ssend.at[k],
+            recv_sem=srecv.at[k],
+            device_id=(group, lax.rem(plane + k, nplane)),
+            device_id_type=MESH,
+        )
+
+    for k in range(1, nplane):
+        spots_to(k).start()
 
     def arrival(i, carry):
         t, side = i // 2, lax.rem(i, 2)
@@ -324,31 +359,14 @@
 
     lax.fori_loop(0, 2 * (ngroup - 1), arrival, 0)
 
-    spots[...] = jnp.zeros_like(spots)
-    for chunk in range(ngroup):
-        spots[chunk : chunk + 1] = raw[chunk, pl.ds(quads * depth * 8, 1)].astype(jnp.int32)
-    own_spots = pltpu.make_async_copy(spots, out_places.at[plane], ssend.at[0])
-    own_spots.start()
-
-    def spots_to(k):
-        return pltpu.make_async_remote_copy(
-            src_ref=spots,
-            dst_ref=out_places.at[plane],
-            send_sem=ssend.at[k],
-            recv_sem=srecv.at[k],
-            device_id=(group, lax.rem(plane + k, nplane)),
-            device_id_type=MESH,
-        )
-
-    for k in range(1, nplane):
-        spots_to(k).start()
-
     for side in range(2):
         for t in range(ngroup - 1):
             inside, copy = along(side, t)
             pl.when(inside)(copy.wait_send)
 
     own_spots.wait()
+    for copy in line:
+        copy.wait_send()
     for k in range(1, nplane):
         spots_to(k).wait_send()
         spots_to(k).wait_recv()
@@ -556,8 +574,10 @@
         out_specs=(anywhere, anywhere),
         scratch_shapes=[
             pltpu.VMEM(brick_data.shape, jnp.float32),
-            pltpu.VMEM((ngroup, (quads * brick + 1) * 8, 128), jnp.float32),
+            pltpu.VMEM((ngroup, quads * brick * 8, 128), jnp.float32),
             pltpu.VMEM((ngroup, nplane, capacity, 8, 128), jnp.float32),
+            pltpu.VMEM((8, 128), jnp.int32),
+            pltpu.VMEM((ngroup, 8, 128), jnp.int32),
             pltpu.VMEM((8, 128), jnp.int32),
             pltpu.SemaphoreType.DMA((2, ngroup - 1)),
             pltpu.SemaphoreType.DMA((2, ngroup - 1)),
@@ -565,6 +585,8 @@
             pltpu.SemaphoreType.DMA((ngroup, nplane)),
             pltpu.SemaphoreType.DMA((nplane,)),
             pltpu.SemaphoreType.DMA((nplane,)),
+            pltpu.SemaphoreType.DMA((ngroup,)),
+            pltpu.SemaphoreType.DMA((ngroup,)),
             pltpu.SemaphoreType.DMA,
         ],
         compiler_params=pltpu.CompilerParams(

time: 50.8 us -> 49.4 us (0.972)
  Pallas kernels: 49.2 us -> 47.8 us
    pallas_call x1, Pallas kernels: 36.2 us -> 34.7 us  [on_device_once(): pl.pallas_call(functools.partial(exchange_kernel, ngroup, nplane, capacit...]
where the time goes in v6:
time: 49.4 us; the launch traced here: 49.1 us
  Pallas kernels  47.8 us (97%)
  between operations  1.28 us (3%)
    pallas_call x1, Pallas kernels, on_device_once(): pl.pallas_call(functools.partial(exchange_kernel, ngroup, nplane, capacit...  34.7 us
    pallas_call x1, Pallas kernels, on_device_once(): pl.pallas_call(functools.partial(spectrum_kernel, nplane, ngroup, capacit...  13.1 us

profile of v6, /device:TPU:0, one launch (start us, length us, event | category | flops | bytes accessed | tf_op | source)
XLA Modules:
  0.0 49.1 jit_solution(1086263005049049374)
XLA Ops:
  1.3 34.7 %exchange.1 = (f32[8,4,16,8,128]{4,3,2,1,0:T(8,128)}, s32[8,8,128]{2,1,0:T(8,128)}) custom-call(f32[4096]{0:T(1024)} %constant.6.clone.coef, s32[1,1]{1,0:T(1,128)S(6)} %copy.10.live, f32[16,16,256]{2,1,0:T(8,128)} %bricks.1, s32[2,16]{1,0:T(2,128)} %xy.1), custom_call_target="tpu_custom_call" | custom-call | tf_op jit(solution)/shard_map/exchange/pallas_call | solution.py:567
  36.0 13.1 %spectrum.1 = (f32[2056,128]{1,0:T(8,128)}, f32[2056,128]{1,0:T(8,128)}) custom-call(s32[8,8,128]{2,1,0:T(8,128)} %get-tuple-element.6.places_hbm, f32[8,4,16,8,128]{4,3,2,1,0:T(8,128)} %get-tuple-element.7.bricks_hbm, bf16[2,544,512]{2,1,0:T(8,128)(2,1)} %constant.7.clone.tx_hbm, bf16[2,2,512,512]{3,2,1,0:T(8,128)(2,1)} %constant.8.clone.ty_hbm), custom_call_target="tpu_custom_call" | custom-call | tf_op jit(solution)/shard_map/spectrum/pallas_call | solution.py:604

commit v7 on v6

--- a/solution.py
+++ b/solution.py
@@ -436,7 +436,7 @@
         loads[1 + chunk].wait()
         lax.fori_loop(0, nplane // 2, lambda pair, carry: (place(chunk, pair), carry)[1], 0)
 
-    batch = 2
+    batch = 4
 
     def arrange(step, carry):
         for h in range(2):

time: 49.4 us -> 50 us (1.012)
  Pallas kernels: 47.8 us -> 48.5 us
    pallas_call x1, Pallas kernels: 13.1 us -> 13.7 us  [on_device_once(): pl.pallas_call(functools.partial(spectrum_kernel, nplane, ngroup, capacit...]
where the time goes in v7:
time: 50 us; the launch traced here: 49.8 us
  Pallas kernels  48.5 us (97%)
  between operations  1.28 us (3%)
    pallas_call x1, Pallas kernels, on_device_once(): pl.pallas_call(functools.partial(exchange_kernel, ngroup, nplane, capacit...  34.7 us
    pallas_call x1, Pallas kernels, on_device_once(): pl.pallas_call(functools.partial(spectrum_kernel, nplane, ngroup, capacit...  13.7 us

profile of v7, /device:TPU:0, one launch (start us, length us, event | category | flops | bytes accessed | tf_op | source)
XLA Modules:
  0.0 49.8 jit_solution(17893372484442083125)
XLA Ops:
  1.3 34.7 %exchange.1 = (f32[8,4,16,8,128]{4,3,2,1,0:T(8,128)}, s32[8,8,128]{2,1,0:T(8,128)}) custom-call(f32[4096]{0:T(1024)} %constant.6.clone.coef, s32[1,1]{1,0:T(1,128)S(6)} %copy.10.live, f32[16,16,256]{2,1,0:T(8,128)} %bricks.1, s32[2,16]{1,0:T(2,128)} %xy.1), custom_call_target="tpu_custom_call" | custom-call | tf_op jit(solution)/shard_map/exchange/pallas_call | solution.py:567
  36.0 13.7 %spectrum.1 = (f32[2056,128]{1,0:T(8,128)}, f32[2056,128]{1,0:T(8,128)}) custom-call(s32[8,8,128]{2,1,0:T(8,128)} %get-tuple-element.6.places_hbm, f32[8,4,16,8,128]{4,3,2,1,0:T(8,128)} %get-tuple-element.7.bricks_hbm, bf16[2,544,512]{2,1,0:T(8,128)(2,1)} %constant.7.clone.tx_hbm, bf16[2,2,512,512]{3,2,1,0:T(8,128)(2,1)} %constant.8.clone.ty_hbm), custom_call_target="tpu_custom_call" | custom-call | tf_op jit(solution)/shard_map/spectrum/pallas_call | solution.py:604
